TPU v7x, 32 devices: a whole 2x2x4 slice. The times are simulated.
32 devices in a mesh: pipe: 8 (over z, core), dp: 2 (over y), tensor: 2 (over x).
Axes of the slice: x: 2, y: 2, z: 4, core: 2. Of those that a mesh axis runs over, the one named last changes fastest.
Arguments:
- ssm_output: bfloat16 [8, 2, 1024, 8192], P('pipe', 'dp', None, 'tensor'), may hold values from -6 to 6
- out_weight: bfloat16 [8, 8192, 4096], P('pipe', 'tensor', 'dp'), may hold values from -0.0625 to 0.0625
- in_weight: bfloat16 [8, 4096, 2048], P('pipe', 'dp', 'tensor'), may hold values from -0.09375 to 0.09375
- gain: float32 [8, 4096], P('pipe'), may hold values from 0.1 to 1.9
- residual: bfloat16 [8, 2, 1024, 4096], P('pipe', 'dp', 'tensor'), may hold values from -1.5 to 1.5
- proj_cotangent: bfloat16 [8, 2, 1024, 2048], P('pipe', 'dp', None, 'tensor'), may hold values from -6 to 6
- stream_cotangent: bfloat16 [8, 2, 1024, 4096], P('pipe', 'dp', 'tensor'), may hold values from -12 to 12
Outputs:
- stream: bfloat16 [8, 2, 1024, 4096], P('pipe', 'dp', 'tensor')
- b_proj: bfloat16 [8, 2, 1024, 2048], P('pipe', 'dp', None, 'tensor')
- residual_grad: bfloat16 [8, 2, 1024, 4096], P('pipe', 'dp', 'tensor')
- gain_grad: float32 [8, 4096], P('pipe')
All inputs are finite; a program needn't handle non-finite values.
Results may differ from a plain program's by a relative error of at most 0.014.
Values may be sent and summed in bfloat16 or wider, within the bound.
A program may use at most 192 MiB of HBM per device.

v0:
```python
import math

import jax
import jax.numpy as jnp
from jax import lax
from jax.sharding import PartitionSpec as P

LAYERS = 118


def shifted(block, axis, distance):
    devices = range(lax.axis_size(axis))
    route = [((i - distance) % len(devices), i) for i in devices]
    return lax.ppermute(block, axis, route)


def body(ssm_output, out_weight, in_weight, gain, residual, proj_cotangent, stream_cotangent):
    depth_scale = 1.0 / math.sqrt(2.0 * LAYERS)
    out_all, in_all = (
        lax.all_gather(out_weight, "dp", axis=2, tiled=True),
        lax.all_gather(in_weight, "dp", axis=1, tiled=True),
    )
    w_out = out_all[0]
    w_in = in_all[0]
    ssm_rows = ssm_output[0]
    gain_row = gain[0]
    resid_rows = residual[0]
    cot_proj = proj_cotangent[0]
    cot_stream = stream_cotangent[0]
    block = ssm_rows
    mixed_sum = jnp.transpose(
        lax.psum_scatter(
            jnp.einsum("mtc,cd->tmd", block, w_out, preferred_element_type=jnp.float32).astype(
                jnp.bfloat16
            ),
            "tensor",
            scatter_dimension=0,
            tiled=True,
        ).astype(jnp.float32),
        (1, 0, 2),
    )
    own_stream = (resid_rows.astype(jnp.float32) + depth_scale * mixed_sum).astype(jnp.bfloat16)
    stream_rows = shifted(own_stream, "pipe", 1)
    stream_f32 = stream_rows.astype(jnp.float32)
    inv_rms = lax.rsqrt(jnp.mean(stream_f32 * stream_f32, axis=-1, keepdims=True) + 1e-05)
    unit_rows = stream_f32 * inv_rms
    normed = (unit_rows * gain_row).astype(jnp.bfloat16)
    projected = jnp.einsum(
        "mtd,dc->mtc",
        lax.all_gather(normed, "tensor", axis=1, tiled=True),
        w_in,
        preferred_element_type=jnp.float32,
    ).astype(jnp.bfloat16)
    block = cot_proj
    normed_grad = jnp.transpose(
        lax.psum_scatter(
            jnp.einsum("mtc,dc->tmd", block, w_in, preferred_element_type=jnp.float32).astype(
                jnp.bfloat16
            ),
            "tensor",
            scatter_dimension=0,
            tiled=True,
        ).astype(jnp.float32),
        (1, 0, 2),
    )
    gain_part = jnp.sum(normed_grad * unit_rows, axis=(0, 1))
    weighted = gain_row * normed_grad
    centre = jnp.mean(weighted * unit_rows, axis=-1, keepdims=True)
    stream_grad = (
        cot_stream.astype(jnp.float32) + inv_rms * (weighted - unit_rows * centre)
    ).astype(jnp.bfloat16)
    resid_grad = shifted(stream_grad, "pipe", -1)
    stream_rows, projected, resid_grad, gain_part = (stream_rows, projected, resid_grad, gain_part)
    gain_total = lax.psum(gain_part, ("dp", "tensor"))
    return (stream_rows[None], projected[None], resid_grad[None], gain_total[None])


def solution(mesh):
    in_specs = (
        P("pipe", "dp", None, "tensor"),
        P("pipe", "tensor", "dp"),
        P("pipe", "dp", "tensor"),
        P("pipe", None),
        P("pipe", "dp", "tensor", None),
        P("pipe", "dp", None, "tensor"),
        P("pipe", "dp", "tensor", None),
    )
    out_specs = (
        P("pipe", "dp", "tensor", None),
        P("pipe", "dp", None, "tensor"),
        P("pipe", "dp", "tensor", None),
        P("pipe", None),
    )
    return jax.shard_map(body, mesh=mesh, in_specs=in_specs, out_specs=out_specs, check_vma=False)
```

profile of v0, /device:TPU:0, one launch (start us, length us, event | category | flops | bytes accessed | tf_op | source)
XLA Modules:
  0.0 847.9 jit_solution(3414313601746256034)
XLA Ops:
  7.2 0.7 all-gather.4.cloned.1.call-update
  8.0 0.7 all-gather.8.cloned.1.call-update
  8.7 392.2 %all-gather.4.cloned.1.call-done = bf16[1,4096,4096]{2,1,0:T(8,128)(2,1)} async-done(((bf16[1,4096,2048]{2,1,0:T(8,128)(2,1)}), bf16[1,4096,4096]{2,1,0:T(8,128)(2,1)}) %all-gather.4.cloned.1.call-update) | async-done | bytes 33554448 | tf_op jit(solution)/shard_map/all_gather | solution.py:20
  400.9 42.6 %convert_bitcast_fusion.1 = bf16[1024,1,4096]{0,2,1:T(8,128)(2,1)} fusion(bf16[1,1,1024,4096]{3,2,1,0:T(8,128)(2,1)} %param.7, bf16[1,4096,4096]{2,1,0:T(8,128)(2,1)} %all-gather.4.cloned.1.call-done), kind=kOutput, calls=%fused_computation.26 | convolution fusion | flops 34363932672 | bytes 50331648 | tf_op jit(solution)/shard_map/mtc,cd->tmd/dot_general | solution.py:33
  443.5 0.2 reduce-scatter.5.cloned.1.call-start
  443.7 62.8 %all-gather.8.cloned.1.call-done = bf16[1,4096,1024]{2,1,0:T(8,128)(2,1)} async-done(((bf16[1,2048,1024]{2,1,0:T(8,128)(2,1)}), bf16[1,4096,1024]{2,1,0:T(8,128)(2,1)}) %all-gather.8.cloned.1.call-update) | async-done | bytes 8388624 | tf_op jit(solution)/shard_map/all_gather | solution.py:21
  506.5 14.6 %convert_bitcast_fusion = bf16[1024,1,4096]{0,2,1:T(8,128)(2,1)} fusion(bf16[1,4096,1024]{2,1,0:T(8,128)(2,1)} %all-gather.8.cloned.1.call-done, bf16[1,1,1024,1024]{3,2,1,0:T(8,128)(2,1)S(1)} %copy-done), kind=kOutput, calls=%fused_computation.25 | convolution fusion | flops 8594128896 | bytes 18874368 | tf_op jit(solution)/shard_map/mtc,dc->tmd/dot_general | solution.py:57
  521.1 6.4 copy.11
  527.6 80.4 %reduce-scatter.3.cloned.1.call-done = bf16[512,1,4096]{0,2,1:T(8,128)(2,1)} async-done(((bf16[1024,1,4096]{0,2,1:T(8,128)(2,1)}), bf16[512,1,4096]{0,2,1:T(8,128)(2,1)}) %reduce-scatter.3.cloned.1.call-update) | async-done | bytes 4194320 | tf_op jit(solution)/shard_map/reduce_scatter | solution.py:32
  608.0 6.7 fusion.13
  614.7 6.4 copy.12
  621.2 43.6 %collective-permute-done = bf16[1,512,4096]{1,2,0:T(8,128)(2,1)} collective-permute-done((bf16[1,512,4096]{1,2,0:T(8,128)(2,1)}, bf16[1,512,4096]{1,2,0:T(8,128)(2,1)}, u32[]{:S(2)}, u32[]{:S(2)}) %collective-permute-start) | collective-permute-done | bytes 4194336 | tf_op jit(solution)/shard_map/ppermute | solution.py:14
  664.8 3.2 fusion.11
  668.0 41.6 %reduce-scatter.5.cloned.1.call-done = bf16[512,1,4096]{0,2,1:T(8,128)(2,1)} async-done(((bf16[1024,1,4096]{0,2,1:T(8,128)(2,1)}), bf16[512,1,4096]{0,2,1:T(8,128)(2,1)}) %reduce-scatter.5.cloned.1.call-update) | async-done | bytes 4194320 | tf_op jit(solution)/shard_map/reduce_scatter | solution.py:56
  709.6 5.5 fusion.12
  715.1 0.4 copy-done.2
  715.5 6.6 fusion.8
  722.1 2.8 collective-permute-start.1
  724.9 6.5 copy.13
  731.4 15.9 %psum.7 = f32[1,4096]{1,0:T(1,128)} all-reduce(f32[1,4096]{1,0:T(1,128)S(1)} %bitcast.56), channel_id=1, replica_groups=mesh['pipe'=8,'dp'=2,'tensor'=2] {'dp','tensor'}, use_global_device_ids=true, to_apply=%region_5.0 | all-reduce | flops 4096 | bytes 32768 | tf_op jit(solution)/shard_map/psum | solution.py:74
  747.3 24.0 %collective-permute-done.1 = bf16[1,512,4096]{1,2,0:T(8,128)(2,1)} collective-permute-done((bf16[1,512,4096]{1,2,0:T(8,128)(2,1)}, bf16[1,512,4096]{1,2,0:T(8,128)(2,1)}, u32[]{:S(2)}, u32[]{:S(2)}) %collective-permute-start.1) | collective-permute-done | bytes 4194336 | tf_op jit(solution)/shard_map/ppermute | solution.py:14
  771.3 6.3 copy.14
  777.6 49.1 %all-gather.6.cloned.1.call-done = bf16[1,1024,4096]{1,2,0:T(8,128)(2,1)} async-done(((bf16[1,512,4096]{1,2,0:T(8,128)(2,1)}), bf16[1,1024,4096]{1,2,0:T(8,128)(2,1)}) %all-gather.6.cloned.1.call-update) | async-done | bytes 8388624 | tf_op jit(solution)/shard_map/all_gather | solution.py:50
  826.7 14.7 %convert_bitcast_fusion.2 = bf16[1,1,1024,1024]{3,2,1,0:T(8,128)(2,1)} fusion(bf16[1,4096,1024]{2,1,0:T(8,128)(2,1)} %all-gather.8.cloned.1.call-done, bf16[1,1024,4096]{1,2,0:T(8,128)(2,1)} %all-gather.6.cloned.1.call-done), kind=kOutput, calls=%fused_computation.28 | convolution fusion | flops 8590983168 | bytes 18874368 | tf_op jit(solution)/shard_map/mtd,dc->mtc/dot_general | solution.py:48
  (17 shorter events, 0.2 us)
Async XLA Ops:
  7.2 499.3 %copy-start = (bf16[1,1,1024,1024]{3,2,1,0:T(8,128)(2,1)S(1)}, bf16[1,1,1024,1024]{3,2,1,0:T(8,128)(2,1)}, u32[]{:S(2)}) copy-start(bf16[1,1,1024,1024]{3,2,1,0:T(8,128)(2,1)} %param.12) | copy-start | bytes 6291460
  7.2 393.7 %all-gather.4.cloned.1.call-start = ((), (), s32[]{:S(2)}) async-start(), calls=%async_computation.2 | async-start | bytes 50331648 | tf_op jit(solution)/shard_map/all_gather | solution.py:20
  7.9 498.5 %all-gather.8.cloned.1.call-start = ((), (), s32[]{:S(2)}) async-start(), calls=%async_computation.5 | async-start | bytes 12582912 | tf_op jit(solution)/shard_map/all_gather | solution.py:21
  8.7 599.4 %reduce-scatter.3.cloned.1.call-start = ((), (), s32[]{:S(2)}) async-start(), calls=%async_computation.3 | async-start | bytes 12582912 | tf_op jit(solution)/shard_map/reduce_scatter | solution.py:32
  443.5 266.1 %reduce-scatter.5.cloned.1.call-start = ((), (), s32[]{:S(2)}) async-start(), calls=%async_computation.6 | async-start | bytes 12582912 | tf_op jit(solution)/shard_map/reduce_scatter | solution.py:56
  521.1 305.6 %all-gather.6.cloned.1.call-start = ((), (), s32[]{:S(2)}) async-start(), calls=%async_computation.4 | async-start | bytes 12582912 | tf_op jit(solution)/shard_map/all_gather | solution.py:50
  614.7 94.8 %copy-start.3 = (f32[1,4096]{1,0:T(1,128)S(1)}, f32[1,4096]{1,0:T(1,128)}, u32[]{:S(2)}) copy-start(f32[1,4096]{1,0:T(1,128)} %param.10) | copy-start | bytes 49156
  614.7 50.0 %collective-permute-start = (bf16[1,512,4096]{1,2,0:T(8,128)(2,1)}, bf16[1,512,4096]{1,2,0:T(8,128)(2,1)}, u32[]{:S(2)}, u32[]{:S(2)}) collective-permute-start(bf16[1,512,4096]{1,2,0:T(8,128)(2,1)} %fusion.13), channel_id=1, source_target_pairs={{28,0},{0,4},{4,8},{8,12},{12,16},{16,20},{20,24},{24,28},{29,1},{... | collective-permute-start | bytes 12582920 | tf_op jit(solution)/shard_map/ppermute | solution.py:14
  709.5 5.6 copy-start.1
  709.5 5.9 copy-start.2
  722.1 49.2 %collective-permute-start.1 = (bf16[1,512,4096]{1,2,0:T(8,128)(2,1)}, bf16[1,512,4096]{1,2,0:T(8,128)(2,1)}, u32[]{:S(2)}, u32[]{:S(2)}) collective-permute-start(bf16[1,512,4096]{1,2,0:T(8,128)(2,1)} %get-tuple-element.10), channel_id=1, source_target_pairs={{4,0},{8,4},{12,8},{16,12},{20,16},{24,20},{28,24},{0,28},{5,1},{9... | collective-permute-start | bytes 12582920 | tf_op jit(solution)/shard_map/ppermute | solution.py:14
Sparse Core Ops, SparseCore 0:
  9.6 391.2 all-gather.3
  402.4 103.9 all-gather.7
  508.7 99.2 reduce-scatter.2
  610.3 99.2 reduce-scatter.4
  722.2 104.4 all-gather.5
where the time goes:
time: 849 us; the launch traced here: 848 us
  waiting for transfers between devices  695 us (82%)
  matrix products  71.9 us (8%)
  local copies, waits for them, and re-layouts  26.1 us (3%)
  other arithmetic  22.1 us (3%)
  blocking collectives  15.9 us (2%)
  between operations  13.8 us (2%)
    all_gather x1, waiting for transfers between devices, body(): lax.all_gather(out_weight, 'dp', axis=2, tiled=True)  392 us
    reduce_scatter x1, waiting for transfers between devices, body(): lax.psum_scatter(jnp.einsum('mtc,cd->tmd', block, w_out, preferred_elemen...  80.4 us
    ppermute x2, waiting for transfers between devices, shifted(): return lax.ppermute(block, axis, route)  67.6 us
    all_gather x1, waiting for transfers between devices, body(): lax.all_gather(in_weight, 'dp', axis=1, tiled=True)  62.8 us
    all_gather x1, waiting for transfers between devices, body(): lax.all_gather(normed, 'tensor', axis=1, tiled=True)  49.1 us
    dot_general x1, matrix products, body(): jnp.einsum('mtc,cd->tmd', block, w_out, preferred_element_type=jnp.float32)  42.6 us
    reduce_scatter x1, waiting for transfers between devices, body(): lax.psum_scatter(jnp.einsum('mtc,dc->tmd', block, w_in, preferred_element...  41.6 us
    unnamed x12, local copies, waits for them, and re-layouts  26.1 us
  transfers between devices with their start and end apart: 7, of which 7 were waited for; matrix products, arithmetic and copies ran while one was open for 11% of the time, Pallas kernels for 0%

commit v1 on v0

--- a/solution.py
+++ b/solution.py
@@ -1,3 +1,4 @@
+import functools
 import math
 
 import jax
@@ -6,6 +7,7 @@
 from jax.sharding import PartitionSpec as P
 
 LAYERS = 118
+PARTS = 4
 
 
 def shifted(block, axis, distance):
@@ -14,7 +16,7 @@
     return lax.ppermute(block, axis, route)
 
 
-def body(ssm_output, out_weight, in_weight, gain, residual, proj_cotangent, stream_cotangent):
+def general_body(ssm_output, out_weight, in_weight, gain, residual, proj_cotangent, stream_cotangent):
     depth_scale = 1.0 / math.sqrt(2.0 * LAYERS)
     out_all, in_all = (
         lax.all_gather(out_weight, "dp", axis=2, tiled=True),
@@ -75,6 +77,89 @@
     return (stream_rows[None], projected[None], resid_grad[None], gain_total[None])
 
 
+def swapped(block, axis):
+    return lax.ppermute(block, axis, [(0, 1), (1, 0)])
+
+
+def after(block, *earlier):
+    return lax.optimization_barrier((block,) + earlier)[0]
+
+
+def paired_body(parts, ssm_output, out_weight, in_weight, gain, residual, proj_cotangent, stream_cotangent):
+    scale = 1.0 / math.sqrt(2.0 * LAYERS)
+    j, k = lax.axis_index("dp"), lax.axis_index("tensor")
+    rows, cot, v, w = ssm_output[0, 0], proj_cotangent[0, 0], in_weight[0], out_weight[0]
+    tokens, half_d = rows.shape[0], w.shape[1]
+    half = tokens // 2
+    step = half // parts
+    gain_row = gain[0]
+    resid, cot_stream = residual[0, 0], stream_cotangent[0, 0]
+    rows_own = lax.dynamic_slice_in_dim(rows, k * half, half, 0)
+    rows_far = lax.dynamic_slice_in_dim(rows, (1 - k) * half, half, 0)
+    cot_own = lax.dynamic_slice_in_dim(cot, k * half, half, 0)
+    cot_far = lax.dynamic_slice_in_dim(cot, (1 - k) * half, half, 0)
+    f32, bf16 = jnp.float32, jnp.bfloat16
+
+    def dot(a, b):
+        return jnp.dot(a, b, preferred_element_type=f32)
+
+    def back(a, b):
+        return lax.dot_general(a, b, (((1,), (1,)), ((), ())), preferred_element_type=f32).astype(bf16)
+
+    def halves(own, far):
+        return jnp.concatenate([jnp.where(j == 0, own, far), jnp.where(j == 0, far, own)], axis=-1)
+
+    v_far = swapped(v, "dp")
+    blocks = rows.reshape(2, parts, step, rows.shape[1])
+    arrived = []
+    for c in range(parts):
+        block = after(blocks[:, c], v_far) if c < 2 else after(blocks[:, c], arrived[c - 2])
+        arrived.append(swapped(block, "dp"))
+    back_own_far = swapped(back(cot_far, v), "tensor")
+    mixed_far = swapped(dot(rows_far, w).astype(bf16), "tensor")
+    mixed_own = dot(rows_own, w).astype(bf16).astype(f32) + mixed_far.astype(f32)
+    grad_own = back(cot_own, v).astype(f32) + back_own_far.astype(f32)
+    back_far_far = swapped(back(cot_far, v_far), "tensor")
+    grad_far = back(cot_own, v_far).astype(f32) + back_far_far.astype(f32)
+    v_all = jnp.concatenate([jnp.where(j == 0, v, v_far), jnp.where(j == 0, v_far, v)], axis=0)
+    streams, grads, near, across = [], [], [], []
+    gain_part = 0.0
+    for c in range(parts):
+        take = slice(c * step, (c + 1) * step)
+        block = arrived[c]
+        to_far = lax.dynamic_index_in_dim(block, 1 - k, 0, keepdims=False)
+        to_own = lax.dynamic_index_in_dim(block, k, 0, keepdims=False)
+        summed = swapped(dot(to_far, w).astype(bf16), "tensor")
+        mixed = (dot(to_own, w).astype(bf16).astype(f32) + summed.astype(f32)).astype(bf16)
+        returned = swapped(mixed, "dp").astype(f32)
+        own_stream = (resid[take].astype(f32) + scale * halves(mixed_own[take], returned)).astype(bf16)
+        stream = shifted(own_stream, "pipe", 1)
+        streams.append(stream)
+        s = stream.astype(f32)
+        inv = lax.rsqrt(jnp.mean(s * s, axis=-1, keepdims=True) + 1e-05)
+        unit = s * inv
+        normed = (unit * gain_row).astype(bf16)
+        normed_far = swapped(normed, "tensor")
+        near.append(dot(normed, v_all).astype(bf16))
+        across.append(dot(normed_far, v_all).astype(bf16))
+        grad = halves(grad_own[take], grad_far[take])
+        gain_part = gain_part + jnp.sum(grad * unit, axis=0)
+        weighted = gain_row * grad
+        centre = jnp.mean(weighted * unit, axis=-1, keepdims=True)
+        out = (cot_stream[take].astype(f32) + inv * (weighted - unit * centre)).astype(bf16)
+        grads.append(shifted(out, "pipe", -1))
+    gain_part = gain_part + swapped(gain_part, "tensor")
+    gain_part = gain_part + swapped(gain_part, "dp")
+    near, across = jnp.concatenate(near, 0), jnp.concatenate(across, 0)
+    projected = jnp.concatenate([jnp.where(k == 0, near, across), jnp.where(k == 0, across, near)], 0)
+    return (
+        jnp.concatenate(streams, 0)[None, None],
+        projected[None, None],
+        jnp.concatenate(grads, 0)[None, None],
+        gain_part[None],
+    )
+
+
 def solution(mesh):
     in_specs = (
         P("pipe", "dp", None, "tensor"),
@@ -91,4 +176,6 @@
         P("pipe", "dp", "tensor", None),
         P("pipe", None),
     )
+    paired = mesh.shape["dp"] == 2 and mesh.shape["tensor"] == 2
+    body = functools.partial(paired_body, PARTS) if paired else general_body
     return jax.shard_map(body, mesh=mesh, in_specs=in_specs, out_specs=out_specs, check_vma=False)

time: 849 us -> 530 us (0.62)
  waiting for transfers between devices: 695 us -> 344 us
  matrix products: 71.9 us -> 108 us
  starting transfers between devices: 3.2 us -> 30.7 us
  local copies, waits for them, and re-layouts: 26.1 us -> 5.09 us
  blocking collectives: 15.9 us -> 0 us
  between operations: 13.8 us -> 1.18 us
  other arithmetic: 22.1 us -> 33.6 us
    all_gather x3 -> x0, waiting for transfers between devices: 504 us -> none  [the longest x1 392 us: body(): lax.all_gather(out_weight, 'dp', axis=2, tiled=True)]
    ppermute x0 -> x22, waiting for transfers between devices: none -> 277 us  [swapped(): return lax.ppermute(block, axis, [(0, 1), (1, 0)])]
    reduce_scatter x2 -> x0, waiting for transfers between devices: 122 us -> none  [the longest x1 80.4 us: body(): lax.psum_scatter(jnp.einsum('mtc,cd->tmd', block, w_out, preferred_elemen...]
    dot_general x3 -> x22, matrix products: 71.9 us -> 108 us  [the longest x18 82.7 us: dot(): return jnp.dot(a, b, preferred_element_type=f32)]
    unnamed x12 -> x26, local copies, waits for them, and re-layouts: 26.1 us -> 1.38 us
    ppermute x0 -> x22, starting transfers between devices: none -> 24.6 us  [swapped(): return lax.ppermute(block, axis, [(0, 1), (1, 0)])]
    psum x1 -> x0, blocking collectives: 15.9 us -> none  [body(): gain_total = lax.psum(gain_part, ('dp', 'tensor'))]
    select_n x0 -> x4, other arithmetic: none -> 13 us  [the longest x1 6.78 us: paired_body(): jnp.where(j == 0, v, v_far)]
  transfers between devices with their start and end apart: 7 -> 30, of which waited for: 7 -> 22; matrix products, arithmetic and copies ran while one was open for 11% -> 23% of each run, Pallas kernels for 0% -> 0%
where the time goes in v1:
time: 530 us; the launch traced here: 523 us
  waiting for transfers between devices  344 us (65%)
  matrix products  108 us (20%)
  other arithmetic  33.6 us (6%)
  starting transfers between devices  30.7 us (6%)
    ppermute x22, waiting for transfers between devices, swapped(): return lax.ppermute(block, axis, [(0, 1), (1, 0)])  277 us
    dot_general x18, matrix products, dot(): return jnp.dot(a, b, preferred_element_type=f32)  82.7 us
    ppermute x8, waiting for transfers between devices, shifted(): return lax.ppermute(block, axis, route)  66.9 us
    dot_general x4, matrix products, back(): lax.dot_general(a, b, (((1,), (1,)), ((), ())), preferred_element_type=f32)  25.1 us
    ppermute x22, starting transfers between devices, swapped(): return lax.ppermute(block, axis, [(0, 1), (1, 0)])  24.6 us
  transfers between devices with their start and end apart: 30, of which 22 were waited for; matrix products, arithmetic and copies ran while one was open for 23% of the time, Pallas kernels for 0%

profile of v1, /device:TPU:0, one launch (start us, length us, event | category | flops | bytes accessed | tf_op | source)
XLA Modules:
  0.0 522.6 jit_solution(10349252929192710180)
XLA Ops:
  0.7 14.7 %fusion.29 = bf16[512,2048]{1,0:T(8,128)(2,1)} fusion(bf16[1,4096,2048]{2,1,0:T(8,128)(2,1)} %param.8, bf16[1,1,1024,4096]{3,2,1,0:T(8,128)(2,1)} %param.7, s32[]{:T(128)S(6)} %select_n.115), kind=kOutput, calls=%fused_computation.33 | convolution fusion | flops 8590983168 | bytes 23068676 | tf_op jit(solution)/shard_map/dot_general | solution.py:104
  19.8 5.9 %convolution_convert_fusion.2 = bf16[512,2048]{1,0:T(8,128)(2,1)} fusion(bf16[1,1,1024,1024]{3,2,1,0:T(8,128)(2,1)S(1)} %copy-done, s32[]{:T(128)S(6)} %select_n.115, bf16[1,2048,1024]{2,1,0:T(8,128)(2,1)} %param.9), kind=kOutput, calls=%fused_computation.36 | convolution fusion | flops 2148532224 | bytes 7340036 | tf_op jit(solution)/shard_map/dot_general | solution.py:107
  30.0 35.1 %collective-permute-done = bf16[512,2048]{1,0:T(8,128)(2,1)} collective-permute-done((bf16[512,2048]{1,0:T(8,128)(2,1)}, bf16[512,2048]{1,0:T(8,128)(2,1)}, u32[]{:S(2)}, u32[]{:S(2)}) %collective-permute-start) | collective-permute-done | bytes 2097184 | tf_op jit(solution)/shard_map/ppermute | solution.py:81
  65.1 25.6 %convert_add_fusion.2 = f32[512,2048]{1,0:T(8,128)S(1)} fusion(bf16[512,2048]{1,0:T(8,128)(2,1)} %collective-permute-done, bf16[1,4096,2048]{2,1,0:T(8,128)(2,1)} %param.8, bf16[1,1,1024,4096]{3,2,1,0:T(8,128)(2,1)} %param.7, s32[]{:T(128)S(6)} %select_n.114), kind=kOutput, calls=%fused_computation.27 | convolution fusion | flops 8594128896 | bytes 27262980 | tf_op jit(solution)/shard_map/dot_general | solution.py:104
  90.7 19.9 %collective-permute-done.1 = bf16[2048,1024]{1,0:T(8,128)(2,1)} collective-permute-done((bf16[2048,1024]{1,0:T(8,128)(2,1)}, bf16[2048,1024]{1,0:T(8,128)(2,1)}, u32[]{:S(2)}, u32[]{:S(2)}) %collective-permute-start.1) | collective-permute-done | bytes 4194336 | tf_op jit(solution)/shard_map/ppermute | solution.py:81
  112.7 7.2 %convert_add_fusion.1 = f32[512,2048]{1,0:T(8,128)} fusion(bf16[512,2048]{1,0:T(8,128)(2,1)} %collective-permute-done.22, bf16[1,1,1024,1024]{3,2,1,0:T(8,128)(2,1)S(1)} %copy-done, s32[]{:T(128)S(6)} %select_n.114, bf16[1,2048,1024]{2,1,0:T(8,128)(2,1)} %param.9), kind=kOutput, calls=%fused_computation.26 | convolution fusion | flops 2151677952 | bytes 11534340 | tf_op jit(solution)/shard_map/dot_general | solution.py:107
  119.9 6.1 %convolution_convert_fusion = bf16[512,2048]{1,0:T(8,128)(2,1)} fusion(bf16[2048,1024]{1,0:T(8,128)(2,1)} %collective-permute-done.1, bf16[1,1,1024,1024]{3,2,1,0:T(8,128)(2,1)S(1)} %copy-done, s32[]{:T(128)S(6)} %select_n.115), kind=kOutput, calls=%fused_computation.34 | convolution fusion | flops 2148532224 | bytes 7340036 | tf_op jit(solution)/shard_map/dot_general | solution.py:107
  126.3 6.8 %broadcast_select_fusion.1 = (bf16[2048,1024]{1,0:T(8,128)(2,1)}, bf16[2048,1024]{1,0:T(8,128)(2,1)}) fusion(bf16[2048,1024]{1,0:T(8,128)(2,1)} %collective-permute-done.1, pred[]{:T(512)S(6)} %eq.4, bf16[1,2048,1024]{2,1,0:T(8,128)(2,1)} %param.9), kind=kLoop, calls=%fused_computation.31 | loop fusion | flops 4194304 | bytes 16777216 | tf_op jit(solution)/shard_map/jit(_where)/select_n | solution.py:124
  133.1 26.2 %collective-permute-done.2 = bf16[2,128,4096]{2,1,0:T(8,128)(2,1)} collective-permute-done((bf16[2,128,4096]{2,1,0:T(8,128)(2,1)S(1)}, bf16[2,128,4096]{2,1,0:T(8,128)(2,1)}, u32[]{:S(2)}, u32[]{:S(2)}) %collective-permute-start.2) | collective-permute-done | bytes 2097184 | tf_op jit(solution)/shard_map/ppermute | solution.py:81
  160.8 43.3 %collective-permute-done.6 = bf16[2,128,4096]{2,1,0:T(8,128)(2,1)S(1)} collective-permute-done((bf16[2,128,4096]{2,1,0:T(8,128)(2,1)S(1)}, bf16[2,128,4096]{2,1,0:T(8,128)(2,1)S(1)}, u32[]{:S(2)}, u32[]{:S(2)}) %collective-permute-start.6) | collective-permute-done | bytes 2097184 | tf_op jit(solution)/shard_map/ppermute | solution.py:81
  217.5 8.0 %collective-permute-done.7 = bf16[128,2048]{1,0:T(8,128)(2,1)} collective-permute-done((bf16[128,2048]{1,0:T(8,128)(2,1)S(1)}, bf16[128,2048]{1,0:T(8,128)(2,1)}, u32[]{:S(2)}, u32[]{:S(2)}) %collective-permute-start.7) | collective-permute-done | bytes 524320 | tf_op jit(solution)/shard_map/ppermute | solution.py:81
  236.9 12.2 %collective-permute-done.10 = bf16[2,128,4096]{2,1,0:T(8,128)(2,1)S(1)} collective-permute-done((bf16[2,128,4096]{2,1,0:T(8,128)(2,1)S(1)}, bf16[2,128,4096]{2,1,0:T(8,128)(2,1)S(1)}, u32[]{:S(2)}, u32[]{:S(2)}) %collective-permute-start.10) | collective-permute-done | bytes 2097184 | tf_op jit(solution)/shard_map/ppermute | solution.py:81
  252.4 41.6 %collective-permute-done.14 = bf16[2,128,4096]{2,1,0:T(8,128)(2,1)S(1)} collective-permute-done((bf16[2,128,4096]{2,1,0:T(8,128)(2,1)S(1)}, bf16[2,128,4096]{2,1,0:T(8,128)(2,1)S(1)}, u32[]{:S(2)}, u32[]{:S(2)}) %collective-permute-start.14) | collective-permute-done | bytes 2097184 | tf_op jit(solution)/shard_map/ppermute | solution.py:81
  309.8 5.9 %convolution_convert_fusion.1 = bf16[512,2048]{1,0:T(8,128)(2,1)} fusion(bf16[2048,1024]{1,0:T(8,128)(2,1)} %collective-permute-done.1, bf16[1,1,1024,1024]{3,2,1,0:T(8,128)(2,1)S(1)} %copy-done, s32[]{:T(128)S(6)} %select_n.114), kind=kOutput, calls=%fused_computation.35 | convolution fusion | flops 2148532224 | bytes 7340036 | tf_op jit(solution)/shard_map/dot_general | solution.py:107
  316.6 11.1 %collective-permute-done.12 = bf16[128,2048]{1,0:T(8,128)(2,1)S(1)} collective-permute-done((bf16[128,2048]{1,0:T(8,128)(2,1)}, bf16[128,2048]{1,0:T(8,128)(2,1)S(1)}, u32[]{:S(2)}, u32[]{:S(2)}) %collective-permute-start.12) | collective-permute-done | bytes 524320 | tf_op jit(solution)/shard_map/ppermute | solution.py:81
  327.7 8.8 %collective-permute-done.16 = bf16[128,2048]{1,0:T(8,128)(2,1)S(1)} collective-permute-done((bf16[128,2048]{1,0:T(8,128)(2,1)S(1)}, bf16[128,2048]{1,0:T(8,128)(2,1)S(1)}, u32[]{:S(2)}, u32[]{:S(2)}) %collective-permute-start.16) | collective-permute-done | bytes 524320 | tf_op jit(solution)/shard_map/ppermute | solution.py:81
  350.7 6.8 %collective-permute-done.17 = bf16[128,4096]{1,0:T(8,128)(2,1)S(1)} collective-permute-done((bf16[128,4096]{1,0:T(8,128)(2,1)}, bf16[128,4096]{1,0:T(8,128)(2,1)S(1)}, u32[]{:S(2)}, u32[]{:S(2)}) %collective-permute-start.17) | collective-permute-done | bytes 1048608 | tf_op jit(solution)/shard_map/ppermute | solution.py:16
  357.8 10.9 %collective-permute-done.13 = bf16[128,4096]{1,0:T(8,128)(2,1)S(1)} collective-permute-done((bf16[128,4096]{1,0:T(8,128)(2,1)}, bf16[128,4096]{1,0:T(8,128)(2,1)S(1)}, u32[]{:S(2)}, u32[]{:S(2)}) %collective-permute-start.13) | collective-permute-done | bytes 1048608 | tf_op jit(solution)/shard_map/ppermute | solution.py:16
  369.0 10.9 %collective-permute-done.9 = bf16[128,4096]{1,0:T(8,128)(2,1)S(1)} collective-permute-done((bf16[128,4096]{1,0:T(8,128)(2,1)}, bf16[128,4096]{1,0:T(8,128)(2,1)S(1)}, u32[]{:S(2)}, u32[]{:S(2)}) %collective-permute-start.9) | collective-permute-done | bytes 1048608 | tf_op jit(solution)/shard_map/ppermute | solution.py:16
  380.3 10.9 %collective-permute-done.5 = bf16[128,4096]{1,0:T(8,128)(2,1)S(1)} collective-permute-done((bf16[128,4096]{1,0:T(8,128)(2,1)S(1)}, bf16[128,4096]{1,0:T(8,128)(2,1)S(1)}, u32[]{:S(2)}, u32[]{:S(2)}) %collective-permute-start.5) | collective-permute-done | bytes 1048608 | tf_op jit(solution)/shard_map/ppermute | solution.py:16
  412.0 58.5 %collective-permute-done.28 = f32[4096]{0:T(1024)S(1)} collective-permute-done((f32[4096]{0:T(1024)S(1)}, f32[4096]{0:T(1024)S(1)}, u32[]{:S(2)}, u32[]{:S(2)}) %collective-permute-start.28) | collective-permute-done | bytes 16416 | tf_op jit(solution)/shard_map/ppermute | solution.py:81
  482.1 7.3 %collective-permute-done.21 = bf16[128,4096]{1,0:T(8,128)(2,1)S(1)} collective-permute-done((bf16[128,4096]{1,0:T(8,128)(2,1)S(1)}, bf16[128,4096]{1,0:T(8,128)(2,1)S(1)}, u32[]{:S(2)}, u32[]{:S(2)}) %collective-permute-start.21) | collective-permute-done | bytes 1048608 | tf_op jit(solution)/shard_map/ppermute | solution.py:81
  497.8 11.2 %collective-permute-done.25 = bf16[128,4096]{1,0:T(8,128)(2,1)S(1)} collective-permute-done((bf16[128,4096]{1,0:T(8,128)(2,1)S(1)}, bf16[128,4096]{1,0:T(8,128)(2,1)S(1)}, u32[]{:S(2)}, u32[]{:S(2)}) %collective-permute-start.25) | collective-permute-done | bytes 1048608 | tf_op jit(solution)/shard_map/ppermute | solution.py:16
  509.1 11.2 %collective-permute-done.27 = bf16[128,4096]{1,0:T(8,128)(2,1)S(1)} collective-permute-done((bf16[128,4096]{1,0:T(8,128)(2,1)S(1)}, bf16[128,4096]{1,0:T(8,128)(2,1)S(1)}, u32[]{:S(2)}, u32[]{:S(2)}) %collective-permute-start.27) | collective-permute-done | bytes 1048608 | tf_op jit(solution)/shard_map/ppermute | solution.py:16
  (111 shorter events, 115.0 us)
Async XLA Ops:
  15.4 49.7 %collective-permute-start = (bf16[512,2048]{1,0:T(8,128)(2,1)}, bf16[512,2048]{1,0:T(8,128)(2,1)}, u32[]{:S(2)}, u32[]{:S(2)}) collective-permute-start(bf16[512,2048]{1,0:T(8,128)(2,1)} %fusion.29), channel_id=1, source_target_pairs={{0,1},{1,0},{2,3},{3,2},{4,5},{5,4},{6,7},{7,6},{8,9},{9,8},{10,11... | collective-permute-start | bytes 6291464 | tf_op jit(solution)/shard_map/ppermute | solution.py:81
  18.3 92.3 %collective-permute-start.1 = (bf16[2048,1024]{1,0:T(8,128)(2,1)}, bf16[2048,1024]{1,0:T(8,128)(2,1)}, u32[]{:S(2)}, u32[]{:S(2)}) collective-permute-start(bf16[2048,1024]{1,0:T(8,128)(2,1)} %bitcast.6), channel_id=1, source_target_pairs={{0,2},{2,0},{1,3},{3,1},{4,6},{6,4},{5,7},{7,5},{8,10},{10,8},{9,1... | collective-permute-start | bytes 12582920 | tf_op jit(solution)/shard_map/ppermute | solution.py:81
  25.7 86.9 %collective-permute-start.22 = (bf16[512,2048]{1,0:T(8,128)(2,1)}, bf16[512,2048]{1,0:T(8,128)(2,1)}, u32[]{:S(2)}, u32[]{:S(2)}) collective-permute-start(bf16[512,2048]{1,0:T(8,128)(2,1)} %convolution_convert_fusion.2), channel_id=1, source_target_pairs={{0,1},{1,0},{2,3},{3,2},{4,5},{5,4},{6,7},{7,6},{8,9},{9,8},{10,11... | collective-permute-start | bytes 6291464 | tf_op jit(solution)/shard_map/ppermute | solution.py:81
  110.6 48.7 %collective-permute-start.2 = (bf16[2,128,4096]{2,1,0:T(8,128)(2,1)S(1)}, bf16[2,128,4096]{2,1,0:T(8,128)(2,1)}, u32[]{:S(2)}, u32[]{:S(2)}) collective-permute-start(bf16[2,128,4096]{2,1,0:T(8,128)(2,1)S(1)} %get-tuple-element.8), channel_id=1, source_target_pairs={{0,2},{2,0},{1,3},{3,1},{4,6},{6,4},{5,7},{7,5},{8,10},{10,8},{9,1... | collective-permute-start | bytes 6291464 | tf_op jit(solution)/shard_map/ppermute | solution.py:81
  112.2 92.0 %collective-permute-start.6 = (bf16[2,128,4096]{2,1,0:T(8,128)(2,1)S(1)}, bf16[2,128,4096]{2,1,0:T(8,128)(2,1)S(1)}, u32[]{:S(2)}, u32[]{:S(2)}) collective-permute-start(bf16[2,128,4096]{2,1,0:T(8,128)(2,1)S(1)} %get-tuple-element.9), channel_id=1, source_target_pairs={{0,2},{2,0},{1,3},{3,1},{4,6},{6,4},{5,7},{7,5},{8,10},{10,8},{9,1... | collective-permute-start | bytes 6291464 | tf_op jit(solution)/shard_map/ppermute | solution.py:81
  126.0 216.9 %collective-permute-start.23 = (bf16[512,2048]{1,0:T(8,128)(2,1)}, bf16[512,2048]{1,0:T(8,128)(2,1)}, u32[]{:S(2)}, u32[]{:S(2)}) collective-permute-start(bf16[512,2048]{1,0:T(8,128)(2,1)} %convolution_convert_fusion), channel_id=1, source_target_pairs={{0,1},{1,0},{2,3},{3,2},{4,5},{5,4},{6,7},{7,6},{8,9},{9,8},{10,11... | collective-permute-start | bytes 6291464 | tf_op jit(solution)/shard_map/ppermute | solution.py:81
  159.3 89.8 %collective-permute-start.10 = (bf16[2,128,4096]{2,1,0:T(8,128)(2,1)S(1)}, bf16[2,128,4096]{2,1,0:T(8,128)(2,1)S(1)}, u32[]{:S(2)}, u32[]{:S(2)}) collective-permute-start(bf16[2,128,4096]{2,1,0:T(8,128)(2,1)S(1)} %get-tuple-element.10), channel_id=1, source_target_pairs={{0,2},{2,0},{1,3},{3,1},{4,6},{6,4},{5,7},{7,5},{8,10},{10,8},{9,1... | collective-permute-start | bytes 6291464 | tf_op jit(solution)/shard_map/ppermute | solution.py:81
  205.5 88.6 %collective-permute-start.14 = (bf16[2,128,4096]{2,1,0:T(8,128)(2,1)S(1)}, bf16[2,128,4096]{2,1,0:T(8,128)(2,1)S(1)}, u32[]{:S(2)}, u32[]{:S(2)}) collective-permute-start(bf16[2,128,4096]{2,1,0:T(8,128)(2,1)S(1)} %get-tuple-element.11), channel_id=1, source_target_pairs={{0,2},{2,0},{1,3},{3,1},{4,6},{6,4},{5,7},{7,5},{8,10},{10,8},{9,1... | collective-permute-start | bytes 6291464 | tf_op jit(solution)/shard_map/ppermute | solution.py:81
  230.2 85.5 %collective-permute-start.8 = (bf16[128,2048]{1,0:T(8,128)(2,1)}, bf16[128,2048]{1,0:T(8,128)(2,1)S(1)}, u32[]{:S(2)}, u32[]{:S(2)}) collective-permute-start(bf16[128,2048]{1,0:T(8,128)(2,1)} %fusion.78), channel_id=1, source_target_pairs={{0,2},{2,0},{1,3},{3,1},{4,6},{6,4},{5,7},{7,5},{8,10},{10,8},{9,1... | collective-permute-start | bytes 1572872 | tf_op jit(solution)/shard_map/ppermute | solution.py:81
  235.8 80.8 %collective-permute-start.4 = (bf16[128,2048]{1,0:T(8,128)(2,1)}, bf16[128,2048]{1,0:T(8,128)(2,1)}, u32[]{:S(2)}, u32[]{:S(2)}) collective-permute-start(bf16[128,2048]{1,0:T(8,128)(2,1)} %fusion.63), channel_id=1, source_target_pairs={{0,2},{2,0},{1,3},{3,1},{4,6},{6,4},{5,7},{7,5},{8,10},{10,8},{9,1... | collective-permute-start | bytes 1572872 | tf_op jit(solution)/shard_map/ppermute | solution.py:81
  252.0 44.9 %collective-permute-start.11 = (bf16[128,2048]{1,0:T(8,128)(2,1)S(1)}, bf16[128,2048]{1,0:T(8,128)(2,1)S(1)}, u32[]{:S(2)}, u32[]{:S(2)}) collective-permute-start(bf16[128,2048]{1,0:T(8,128)(2,1)S(1)} %fusion.96), channel_id=1, source_target_pairs={{0,1},{1,0},{2,3},{3,2},{4,5},{5,4},{6,7},{7,6},{8,9},{9,8},{10,11... | collective-permute-start | bytes 1572872 | tf_op jit(solution)/shard_map/ppermute | solution.py:81
  300.2 27.6 %collective-permute-start.12 = (bf16[128,2048]{1,0:T(8,128)(2,1)}, bf16[128,2048]{1,0:T(8,128)(2,1)S(1)}, u32[]{:S(2)}, u32[]{:S(2)}) collective-permute-start(bf16[128,2048]{1,0:T(8,128)(2,1)} %fusion.93), channel_id=1, source_target_pairs={{0,2},{2,0},{1,3},{3,1},{4,6},{6,4},{5,7},{7,5},{8,10},{10,8},{9,1... | collective-permute-start | bytes 1572872 | tf_op jit(solution)/shard_map/ppermute | solution.py:81
  308.2 28.4 %collective-permute-start.16 = (bf16[128,2048]{1,0:T(8,128)(2,1)S(1)}, bf16[128,2048]{1,0:T(8,128)(2,1)S(1)}, u32[]{:S(2)}, u32[]{:S(2)}) collective-permute-start(bf16[128,2048]{1,0:T(8,128)(2,1)S(1)} %fusion.108), channel_id=1, source_target_pairs={{0,2},{2,0},{1,3},{3,1},{4,6},{6,4},{5,7},{7,5},{8,10},{10,8},{9,1... | collective-permute-start | bytes 1572872 | tf_op jit(solution)/shard_map/ppermute | solution.py:81
  341.3 27.5 %collective-permute-start.13 = (bf16[128,4096]{1,0:T(8,128)(2,1)}, bf16[128,4096]{1,0:T(8,128)(2,1)S(1)}, u32[]{:S(2)}, u32[]{:S(2)}) collective-permute-start(bf16[128,4096]{1,0:T(8,128)(2,1)} %get-tuple-element.48), channel_id=1, source_target_pairs={{28,0},{0,4},{4,8},{8,12},{12,16},{16,20},{20,24},{24,28},{29,1},{... | collective-permute-start | bytes 3145736 | tf_op jit(solution)/shard_map/ppermute | solution.py:16
  345.3 34.6 %collective-permute-start.9 = (bf16[128,4096]{1,0:T(8,128)(2,1)}, bf16[128,4096]{1,0:T(8,128)(2,1)S(1)}, u32[]{:S(2)}, u32[]{:S(2)}) collective-permute-start(bf16[128,4096]{1,0:T(8,128)(2,1)} %get-tuple-element.46), channel_id=1, source_target_pairs={{28,0},{0,4},{4,8},{8,12},{12,16},{16,20},{20,24},{24,28},{29,1},{... | collective-permute-start | bytes 3145736 | tf_op jit(solution)/shard_map/ppermute | solution.py:16
  349.1 42.1 %collective-permute-start.5 = (bf16[128,4096]{1,0:T(8,128)(2,1)S(1)}, bf16[128,4096]{1,0:T(8,128)(2,1)S(1)}, u32[]{:S(2)}, u32[]{:S(2)}) collective-permute-start(bf16[128,4096]{1,0:T(8,128)(2,1)S(1)} %copy-done.7), channel_id=1, source_target_pairs={{28,0},{0,4},{4,8},{8,12},{12,16},{16,20},{20,24},{24,28},{29,1},{... | collective-permute-start | bytes 3145736 | tf_op jit(solution)/shard_map/ppermute | solution.py:16
  398.9 76.0 %collective-permute-start.18 = (bf16[128,4096]{1,0:T(8,128)(2,1)}, bf16[128,4096]{1,0:T(8,128)(2,1)S(1)}, u32[]{:S(2)}, u32[]{:S(2)}) collective-permute-start(bf16[128,4096]{1,0:T(8,128)(2,1)} %get-tuple-element.59), channel_id=1, source_target_pairs={{0,1},{1,0},{2,3},{3,2},{4,5},{5,4},{6,7},{7,6},{8,9},{9,8},{10,11... | collective-permute-start | bytes 3145736 | tf_op jit(solution)/shard_map/ppermute | solution.py:81
  403.9 74.4 %collective-permute-start.19 = (bf16[128,4096]{1,0:T(8,128)(2,1)S(1)}, bf16[128,4096]{1,0:T(8,128)(2,1)S(1)}, u32[]{:S(2)}, u32[]{:S(2)}) collective-permute-start(bf16[128,4096]{1,0:T(8,128)(2,1)S(1)} %get-tuple-element.57), channel_id=1, source_target_pairs={{0,1},{1,0},{2,3},{3,2},{4,5},{5,4},{6,7},{7,6},{8,9},{9,8},{10,11... | collective-permute-start | bytes 3145736 | tf_op jit(solution)/shard_map/ppermute | solution.py:81
  407.7 72.2 %collective-permute-start.20 = (bf16[128,4096]{1,0:T(8,128)(2,1)S(1)}, bf16[128,4096]{1,0:T(8,128)(2,1)S(1)}, u32[]{:S(2)}, u32[]{:S(2)}) collective-permute-start(bf16[128,4096]{1,0:T(8,128)(2,1)S(1)} %get-tuple-element.61), channel_id=1, source_target_pairs={{0,1},{1,0},{2,3},{3,2},{4,5},{5,4},{6,7},{7,6},{8,9},{9,8},{10,11... | collective-permute-start | bytes 3145736 | tf_op jit(solution)/shard_map/ppermute | solution.py:81
  408.4 62.1 %collective-permute-start.28 = (f32[4096]{0:T(1024)S(1)}, f32[4096]{0:T(1024)S(1)}, u32[]{:S(2)}, u32[]{:S(2)}) collective-permute-start(f32[4096]{0:T(1024)S(1)} %add_add_fusion), channel_id=1, source_target_pairs={{0,1},{1,0},{2,3},{3,2},{4,5},{5,4},{6,7},{7,6},{8,9},{9,8},{10,11... | collective-permute-start | bytes 49160 | tf_op jit(solution)/shard_map/ppermute | solution.py:81
  411.3 78.0 %collective-permute-start.21 = (bf16[128,4096]{1,0:T(8,128)(2,1)S(1)}, bf16[128,4096]{1,0:T(8,128)(2,1)S(1)}, u32[]{:S(2)}, u32[]{:S(2)}) collective-permute-start(bf16[128,4096]{1,0:T(8,128)(2,1)S(1)} %get-tuple-element.58), channel_id=1, source_target_pairs={{0,1},{1,0},{2,3},{3,2},{4,5},{5,4},{6,7},{7,6},{8,9},{9,8},{10,11... | collective-permute-start | bytes 3145736 | tf_op jit(solution)/shard_map/ppermute | solution.py:81
  474.9 22.9 %collective-permute-start.24 = (bf16[128,4096]{1,0:T(8,128)(2,1)S(1)}, bf16[128,4096]{1,0:T(8,128)(2,1)S(1)}, u32[]{:S(2)}, u32[]{:S(2)}) collective-permute-start(bf16[128,4096]{1,0:T(8,128)(2,1)S(1)} %get-tuple-element.42), channel_id=1, source_target_pairs={{4,0},{8,4},{12,8},{16,12},{20,16},{24,20},{28,24},{0,28},{5,1},{9... | collective-permute-start | bytes 3145736 | tf_op jit(solution)/shard_map/ppermute | solution.py:16
  478.3 30.7 %collective-permute-start.25 = (bf16[128,4096]{1,0:T(8,128)(2,1)S(1)}, bf16[128,4096]{1,0:T(8,128)(2,1)S(1)}, u32[]{:S(2)}, u32[]{:S(2)}) collective-permute-start(bf16[128,4096]{1,0:T(8,128)(2,1)S(1)} %get-tuple-element.43), channel_id=1, source_target_pairs={{4,0},{8,4},{12,8},{16,12},{20,16},{24,20},{28,24},{0,28},{5,1},{9... | collective-permute-start | bytes 3145736 | tf_op jit(solution)/shard_map/ppermute | solution.py:16
  480.0 40.3 %collective-permute-start.27 = (bf16[128,4096]{1,0:T(8,128)(2,1)S(1)}, bf16[128,4096]{1,0:T(8,128)(2,1)S(1)}, u32[]{:S(2)}, u32[]{:S(2)}) collective-permute-start(bf16[128,4096]{1,0:T(8,128)(2,1)S(1)} %get-tuple-element.44), channel_id=1, source_target_pairs={{4,0},{8,4},{12,8},{16,12},{20,16},{24,20},{28,24},{0,28},{5,1},{9... | collective-permute-start | bytes 3145736 | tf_op jit(solution)/shard_map/ppermute | solution.py:16
  (19 other events, 520.0 us)

commit v2 on v0

--- a/solution.py
+++ b/solution.py
@@ -1,3 +1,4 @@
+import functools
 import math
 
 import jax
@@ -6,6 +7,7 @@
 from jax.sharding import PartitionSpec as P
 
 LAYERS = 118
+SHARES = (2, 2, 2, 1, 1)
 
 
 def shifted(block, axis, distance):
@@ -14,7 +16,7 @@
     return lax.ppermute(block, axis, route)
 
 
-def body(ssm_output, out_weight, in_weight, gain, residual, proj_cotangent, stream_cotangent):
+def general_body(ssm_output, out_weight, in_weight, gain, residual, proj_cotangent, stream_cotangent):
     depth_scale = 1.0 / math.sqrt(2.0 * LAYERS)
     out_all, in_all = (
         lax.all_gather(out_weight, "dp", axis=2, tiled=True),
@@ -75,6 +77,152 @@
     return (stream_rows[None], projected[None], resid_grad[None], gain_total[None])
 
 
+def swapped(block, axis):
+    return lax.ppermute(block, axis, [(0, 1), (1, 0)])
+
+
+class Order:
+    def __init__(self):
+        self.last = None
+
+    def step(self, fn, *args):
+        if self.last is not None:
+            args = lax.optimization_barrier(args + (self.last,))[:-1]
+        out = fn(*args)
+        self.last = out[0] if isinstance(out, tuple) else out
+        return out
+
+
+def paired_body(shares, ssm_output, out_weight, in_weight, gain, residual, proj_cotangent, stream_cotangent):
+    scale = 1.0 / math.sqrt(2.0 * LAYERS)
+    j, k = lax.axis_index("dp"), lax.axis_index("tensor")
+    rows, cot, v, w = ssm_output[0, 0], proj_cotangent[0, 0], in_weight[0], out_weight[0]
+    tokens = rows.shape[0]
+    half = tokens // 2
+    unit_rows = half // sum(shares)
+    bounds = [unit_rows * sum(shares[:i]) for i in range(len(shares) + 1)]
+    takes = [slice(a, b) for a, b in zip(bounds, bounds[1:])]
+    gain_row = gain[0]
+    resid, cot_stream = residual[0, 0], stream_cotangent[0, 0]
+    f32, bf16 = jnp.float32, jnp.bfloat16
+
+    def mine(x):
+        return lax.dynamic_slice_in_dim(x, k * half, half, 0)
+
+    def others(x):
+        return lax.dynamic_slice_in_dim(x, (1 - k) * half, half, 0)
+
+    def dot(a, b):
+        return jnp.dot(a, b, preferred_element_type=f32).astype(bf16)
+
+    def back(a, b):
+        return lax.dot_general(a, b, (((1,), (1,)), ((), ())), preferred_element_type=f32).astype(bf16)
+
+    def halves(own, far):
+        return jnp.concatenate([jnp.where(j == 0, own, far), jnp.where(j == 0, far, own)], axis=-1)
+
+    def add(a, b):
+        return a.astype(f32) + b.astype(f32)
+
+    order = Order()
+    count = len(takes)
+    paired = rows.reshape(2, half, rows.shape[1])
+    v_far = swapped(v, "dp")
+    arrived, got = [], {}
+
+    def send(c):
+        block = paired[:, takes[c]]
+        gate = None if c == 0 else v_far if c == 1 else arrived[c - 2]
+        if gate is not None:
+            block = lax.optimization_barrier((block, gate))[0]
+        arrived.append(swapped(block, "dp"))
+
+    send(0)
+    back_near = swapped(order.step(lambda a, b: back(others(a), b), cot, v), "tensor")
+    mixed_near = swapped(order.step(lambda a, b: dot(others(a), b), rows, w), "tensor")
+    mixed_own = order.step(lambda a, b: dot(mine(a), b), rows, w)
+    back_own = order.step(lambda a, b: back(mine(a), b), cot, v)
+    back_away = swapped(order.step(lambda a, b: back(others(a), b), cot, v_far), "tensor")
+    send(1)
+    back_far = order.step(lambda a, b: back(mine(a), b), cot, v_far)
+    v_all = order.step(
+        lambda a, b: jnp.concatenate([jnp.where(j == 0, a, b), jnp.where(j == 0, b, a)], axis=0), v, v_far
+    )
+    summed, kept, returned, stream, normed, grads, near, across = {}, {}, {}, {}, {}, {}, {}, {}
+    gain_part = None
+
+    def multiply(c):
+        half_of = lambda x, i: lax.dynamic_index_in_dim(x, i, 0, keepdims=False)
+        summed[c] = swapped(order.step(lambda x: dot(half_of(x, 1 - k), w), arrived[c]), "tensor")
+        if c + 2 < count:
+            send(c + 2)
+        kept[c] = order.step(lambda x: dot(half_of(x, k), w), arrived[c])
+
+    def give_back(c):
+        returned[c] = swapped(order.step(lambda a, b: add(a, b).astype(bf16), kept[c], summed[c]), "dp")
+
+    def finish_stream(c):
+        t = takes[c]
+
+        def fn(back_half, own, far, res):
+            total = halves(add(own[t], far[t]), back_half.astype(f32))
+            return (res[t].astype(f32) + scale * total).astype(bf16)
+
+        stream[c] = shifted(order.step(fn, returned[c], mixed_own, mixed_near, resid), "pipe", 1)
+
+    def normalise(c):
+        nonlocal gain_part
+        t = takes[c]
+
+        def norm(s):
+            s = s.astype(f32)
+            inv = lax.rsqrt(jnp.mean(s * s, axis=-1, keepdims=True) + 1e-05)
+            return ((s * inv) * gain_row).astype(bf16), inv
+
+        normed[c], inv = order.step(norm, stream[c])
+        got[c] = swapped(normed[c], "tensor")
+
+        def finish(s, inv, own, own_in, far, far_in, cots):
+            unit = s.astype(f32) * inv
+            grad = halves(add(own[t], own_in[t]), add(far[t], far_in[t]))
+            gains = jnp.sum(grad * unit, axis=0)
+            weighted = gain_row * grad
+            centre = jnp.mean(weighted * unit, axis=-1, keepdims=True)
+            return (cots[t].astype(f32) + inv * (weighted - unit * centre)).astype(bf16), gains
+
+        out, gains = order.step(
+            finish, stream[c], inv, back_own, back_near, back_far, back_away, cot_stream
+        )
+        gain_part = gains if gain_part is None else gain_part + gains
+        grads[c] = shifted(out, "pipe", -1)
+
+    def project(c):
+        near[c] = order.step(dot, normed[c], v_all)
+        across[c] = order.step(dot, got[c], v_all)
+
+    for i in range(count + 2):
+        if i < count:
+            multiply(i)
+        if 1 <= i <= count:
+            finish_stream(i - 1)
+        if 2 <= i:
+            project(i - 2)
+        if i < count:
+            give_back(i)
+        if 1 <= i <= count:
+            normalise(i - 1)
+            if i == count:
+                gain_part = gain_part + swapped(gain_part, "tensor")
+                gain_part = gain_part + swapped(gain_part, "dp")
+
+    def joined(parts):
+        return jnp.concatenate([parts[c] for c in range(count)], 0)
+
+    low, high = joined(near), joined(across)
+    projected = jnp.concatenate([jnp.where(k == 0, low, high), jnp.where(k == 0, high, low)], 0)
+    return joined(stream)[None, None], projected[None, None], joined(grads)[None, None], gain_part[None]
+
+
 def solution(mesh):
     in_specs = (
         P("pipe", "dp", None, "tensor"),
@@ -91,4 +239,6 @@
         P("pipe", "dp", "tensor", None),
         P("pipe", None),
     )
+    paired = mesh.shape["dp"] == 2 and mesh.shape["tensor"] == 2
+    body = functools.partial(paired_body, SHARES) if paired else general_body
     return jax.shard_map(body, mesh=mesh, in_specs=in_specs, out_specs=out_specs, check_vma=False)

time: 849 us -> 468 us (0.55)
  waiting for transfers between devices: 695 us -> 220 us
  matrix products: 71.9 us -> 120 us
  other arithmetic: 22.1 us -> 60.4 us
  starting transfers between devices: 3.2 us -> 39.6 us
  blocking collectives: 15.9 us -> 0 us
  between operations: 13.8 us -> 1.69 us
    all_gather x3 -> x0, waiting for transfers between devices: 504 us -> none  [the longest x1 392 us: body(): lax.all_gather(out_weight, 'dp', axis=2, tiled=True)]
    ppermute x0 -> x26, waiting for transfers between devices: none -> 176 us  [swapped(): return lax.ppermute(block, axis, [(0, 1), (1, 0)])]
    reduce_scatter x2 -> x0, waiting for transfers between devices: 122 us -> none  [the longest x1 80.4 us: body(): lax.psum_scatter(jnp.einsum('mtc,cd->tmd', block, w_out, preferred_elemen...]
    dot_general x3 -> x26, matrix products: 71.9 us -> 120 us  [the longest x22 96.2 us: dot(): return jnp.dot(a, b, preferred_element_type=f32).astype(bf16)]
    ppermute x0 -> x26, starting transfers between devices: none -> 30.2 us  [swapped(): return lax.ppermute(block, axis, [(0, 1), (1, 0)])]
    ppermute x2 -> x10, waiting for transfers between devices: 67.6 us -> 44.3 us  [shifted(): return lax.ppermute(block, axis, route)]
    select_n x0 -> x12, other arithmetic: none -> 21 us  [the longest x10 15.5 us: halves(): jnp.where(j == 0, own, far)]
    unnamed x12 -> x42, local copies, waits for them, and re-layouts: 26.1 us -> 8.04 us
  transfers between devices with their start and end apart: 7 -> 36, of which waited for: 7 -> 16; matrix products, arithmetic and copies ran while one was open for 11% -> 42% of each run, Pallas kernels for 0% -> 0%
where the time goes in v2:
time: 468 us; the launch traced here: 461 us
  waiting for transfers between devices  220 us (47%)
  matrix products  120 us (26%)
  other arithmetic  60.4 us (13%)
  starting transfers between devices  39.6 us (8%)
  local copies, waits for them, and re-layouts  18.6 us (4%)
    ppermute x26, waiting for transfers between devices, swapped(): return lax.ppermute(block, axis, [(0, 1), (1, 0)])  176 us
    dot_general x22, matrix products, dot(): return jnp.dot(a, b, preferred_element_type=f32).astype(bf16)  96.2 us
    ppermute x10, waiting for transfers between devices, shifted(): return lax.ppermute(block, axis, route)  44.3 us
    ppermute x26, starting transfers between devices, swapped(): return lax.ppermute(block, axis, [(0, 1), (1, 0)])  30.2 us
    dot_general x4, matrix products, back(): lax.dot_general(a, b, (((1,), (1,)), ((), ())), preferred_element_type=f32)  24.1 us
    select_n x10, other arithmetic, halves(): jnp.where(j == 0, own, far)  15.5 us
    convert_element_type x5, other arithmetic, finish(): (cots[t].astype(f32) + inv * (weighted - unit * centre)).astype(bf16)  11.7 us
    ppermute x10, starting transfers between devices, shifted(): return lax.ppermute(block, axis, route)  9.44 us
  transfers between devices with their start and end apart: 36, of which 16 were waited for; matrix products, arithmetic and copies ran while one was open for 42% of the time, Pallas kernels for 0%

profile of v2, /device:TPU:0, one launch (start us, length us, event | category | flops | bytes accessed | tf_op | source)
XLA Modules:
  0.0 460.7 jit_solution(12150594463080676666)
XLA Ops:
  3.7 5.8 %fusion.104 = (bf16[2,128,4096]{2,1,0:T(8,128)(2,1)}, bf16[2,128,4096]{2,1,0:T(8,128)(2,1)}, bf16[2,128,4096]{2,1,0:T(8,128)(2,1)}) fusion(bf16[2,512,4096]{2,1,0:T(8,128)(2,1)} %bitcast.119), kind=kLoop, calls=%fused_computation.230 | loop fusion | bytes 12582912 | tf_op jit(solution)/shard_map/slice | solution.py:134
  9.6 6.1 %convolution_convert_fusion.3 = bf16[512,2048]{1,0:T(8,128)(2,1)} fusion(bf16[1,1,1024,1024]{3,2,1,0:T(8,128)(2,1)S(1)} %copy-done, s32[]{:T(128)S(6)} %select_n.139, bf16[1,2048,1024]{2,1,0:T(8,128)(2,1)} %param.9), kind=kOutput, calls=%fused_computation.12 | convolution fusion | flops 2148532224 | bytes 7340036 | tf_op jit(solution)/shard_map/dot_general | solution.py:119
  17.6 13.3 %fusion.4 = bf16[512,2048]{1,0:T(8,128)(2,1)} fusion(bf16[4096,2048]{1,0:T(8,128)(2,1)} %bitcast.111, bf16[1024,4096]{1,0:T(8,128)(2,1)S(1)} %bitcast.122, s32[]{:T(128)S(6)} %select_n.139), kind=kOutput, calls=%fused_computation.7 | convolution fusion | flops 8590983168 | bytes 23068676 | tf_op jit(solution)/shard_map/dot_general | solution.py:116
  31.1 14.8 %fusion.7 = bf16[512,2048]{1,0:T(8,128)(2,1)} fusion(bf16[4096,2048]{1,0:T(8,128)(2,1)} %bitcast.112, bf16[1024,4096]{1,0:T(8,128)(2,1)} %bitcast.120, s32[]{:T(128)S(6)} %select_n.140), kind=kOutput, calls=%fused_computation.8 | convolution fusion | flops 8590983168 | bytes 23068676 | tf_op jit(solution)/shard_map/dot_general | solution.py:116
  45.8 6.0 %convolution_convert_fusion.2 = bf16[512,2048]{1,0:T(8,128)(2,1)} fusion(bf16[2048,1024]{1,0:T(8,128)(2,1)} %bitcast.124, bf16[1024,1024]{1,0:T(8,128)(2,1)S(1)} %bitcast.108, s32[]{:T(128)S(6)} %select_n.140), kind=kOutput, calls=%fused_computation.11 | convolution fusion | flops 2148532224 | bytes 7340036 | tf_op jit(solution)/shard_map/dot_general | solution.py:119
  51.8 87.7 %collective-permute-done = bf16[2,128,4096]{2,1,0:T(8,128)(2,1)} collective-permute-done((bf16[2,128,4096]{2,1,0:T(8,128)(2,1)}, bf16[2,128,4096]{2,1,0:T(8,128)(2,1)}, u32[]{:S(2)}, u32[]{:S(2)}) %collective-permute-start) | collective-permute-done | bytes 2097184 | tf_op jit(solution)/shard_map/ppermute | solution.py:81
  141.3 5.9 %convolution_convert_fusion.1 = bf16[512,2048]{1,0:T(8,128)(2,1)} fusion(bf16[2048,1024]{1,0:T(8,128)(2,1)} %collective-permute-done.1, bf16[1024,1024]{1,0:T(8,128)(2,1)S(1)} %bitcast.109, s32[]{:T(128)S(6)} %select_n.139), kind=kOutput, calls=%fused_computation.10 | convolution fusion | flops 2148532224 | bytes 7340036 | tf_op jit(solution)/shard_map/dot_general | solution.py:119
  147.2 6.1 %convolution_convert_fusion = bf16[512,2048]{1,0:T(8,128)(2,1)} fusion(bf16[2048,1024]{1,0:T(8,128)(2,1)} %collective-permute-done.1, bf16[1024,1024]{1,0:T(8,128)(2,1)S(1)} %bitcast.110, s32[]{:T(128)S(6)} %select_n.140), kind=kOutput, calls=%fused_computation.9 | convolution fusion | flops 2148532224 | bytes 7340036 | tf_op jit(solution)/shard_map/dot_general | solution.py:119
  153.3 5.4 %broadcast_select_fusion.1 = (bf16[2048,1024]{1,0:T(8,128)(2,1)}, bf16[2048,1024]{1,0:T(8,128)(2,1)}) fusion(bf16[2048,1024]{1,0:T(8,128)(2,1)S(1)} %bitcast.125, bf16[2048,1024]{1,0:T(8,128)(2,1)} %collective-permute-done.1, pred[]{:T(512)S(6)} %eq.4), kind=kLoop, calls=%fused_computation.6 | loop fusion | flops 4194304 | bytes 16777216 | tf_op jit(solution)/shard_map/jit(_where)/select_n | solution.py:149
  158.7 7.7 %pad_maximum_fusion = bf16[4096,1024]{1,0:T(8,128)(2,1)} fusion(bf16[2048,1024]{1,0:T(8,128)(2,1)} %get-tuple-element.262, bf16[2048,1024]{1,0:T(8,128)(2,1)} %get-tuple-element.261), kind=kLoop, calls=%fused_computation | loop fusion | flops 16777216 | bytes 16777216 | tf_op jit(solution)/shard_map/concatenate | solution.py:149
  166.7 8.6 %convolution_convert_fusion.9 = bf16[128,2048]{1,0:T(8,128)(2,1)S(1)} fusion(bf16[2,128,4096]{2,1,0:T(8,128)(2,1)} %collective-permute-done, s32[]{:T(128)S(6)} %select_n.143, bf16[1,4096,2048]{2,1,0:T(8,128)(2,1)} %param.8), kind=kOutput, calls=%fused_computation.24 | convolution fusion | flops 2147745792 | bytes 18350084 | tf_op jit(solution)/shard_map/dot_general | solution.py:116
  177.1 9.1 %convolution_convert_fusion.8 = bf16[128,2048]{1,0:T(8,128)(2,1)S(1)} fusion(bf16[2,128,4096]{2,1,0:T(8,128)(2,1)} %collective-permute-done, s32[]{:T(128)S(6)} %select_n.144, bf16[1,4096,2048]{2,1,0:T(8,128)(2,1)} %param.8), kind=kOutput, calls=%fused_computation.23 | convolution fusion | flops 2147745792 | bytes 18350084 | tf_op jit(solution)/shard_map/dot_general | solution.py:116
  189.4 42.0 %collective-permute-done.5 = bf16[2,128,4096]{2,1,0:T(8,128)(2,1)S(1)} collective-permute-done((bf16[2,128,4096]{2,1,0:T(8,128)(2,1)}, bf16[2,128,4096]{2,1,0:T(8,128)(2,1)S(1)}, u32[]{:S(2)}, u32[]{:S(2)}) %collective-permute-start.5) | collective-permute-done | bytes 2097184 | tf_op jit(solution)/shard_map/ppermute | solution.py:81
  239.5 4.3 collective-permute-done.3
  254.4 9.9 %collective-permute-done.6 = bf16[128,4096]{1,0:T(8,128)(2,1)S(1)} collective-permute-done((bf16[128,4096]{1,0:T(8,128)(2,1)}, bf16[128,4096]{1,0:T(8,128)(2,1)S(1)}, u32[]{:S(2)}, u32[]{:S(2)}) %collective-permute-start.6) | collective-permute-done | bytes 1048608 | tf_op jit(solution)/shard_map/ppermute | solution.py:16
  273.5 9.4 %convolution_convert_fusion.5 = bf16[128,2048]{1,0:T(8,128)(2,1)} fusion(bf16[2,128,4096]{2,1,0:T(8,128)(2,1)} %collective-permute-done.9, s32[]{:T(128)S(6)} %select_n.143, bf16[1,4096,2048]{2,1,0:T(8,128)(2,1)} %param.8), kind=kOutput, calls=%fused_computation.20 | convolution fusion | flops 2147745792 | bytes 18350084 | tf_op jit(solution)/shard_map/dot_general | solution.py:116
  288.5 22.4 %collective-permute-done.8 = bf16[128,2048]{1,0:T(8,128)(2,1)S(1)} collective-permute-done((bf16[128,2048]{1,0:T(8,128)(2,1)S(1)}, bf16[128,2048]{1,0:T(8,128)(2,1)S(1)}, u32[]{:S(2)}, u32[]{:S(2)}) %collective-permute-start.8) | collective-permute-done | bytes 524320 | tf_op jit(solution)/shard_map/ppermute | solution.py:81
  322.9 11.7 %collective-permute-done.29 = bf16[128,4096]{1,0:T(8,128)(2,1)S(1)} collective-permute-done((bf16[128,4096]{1,0:T(8,128)(2,1)}, bf16[128,4096]{1,0:T(8,128)(2,1)S(1)}, u32[]{:S(2)}, u32[]{:S(2)}) %collective-permute-start.29) | collective-permute-done | bytes 1048608 | tf_op jit(solution)/shard_map/ppermute | solution.py:16
  346.1 4.1 convolution_convert_fusion.13
  351.4 4.1 convolution_convert_fusion.12
  371.8 4.2 collective-permute-done.17
  388.5 4.1 convolution_convert_fusion.10
  401.4 9.8 %collective-permute-done.22 = bf16[64,4096]{1,0:T(8,128)(2,1)S(1)} collective-permute-done((bf16[64,4096]{1,0:T(8,128)(2,1)S(1)}, bf16[64,4096]{1,0:T(8,128)(2,1)S(1)}, u32[]{:S(2)}, u32[]{:S(2)}) %collective-permute-start.22) | collective-permute-done | bytes 524320 | tf_op jit(solution)/shard_map/ppermute | solution.py:16
  442.2 9.6 %collective-permute-done.34 = f32[4096]{0:T(1024)S(1)} collective-permute-done((f32[4096]{0:T(1024)S(1)}, f32[4096]{0:T(1024)S(1)}, u32[]{:S(2)}, u32[]{:S(2)}) %collective-permute-start.34) | collective-permute-done | bytes 16416 | tf_op jit(solution)/shard_map/ppermute | solution.py:81
  (180 shorter events, 147.0 us)
Async XLA Ops:
  0.6 140.6 %collective-permute-start.1 = (bf16[2048,1024]{1,0:T(8,128)(2,1)}, bf16[2048,1024]{1,0:T(8,128)(2,1)}, u32[]{:S(2)}, u32[]{:S(2)}) collective-permute-start(bf16[2048,1024]{1,0:T(8,128)(2,1)} %bitcast.123), channel_id=1, source_target_pairs={{0,2},{2,0},{1,3},{3,1},{4,6},{6,4},{5,7},{7,5},{8,10},{10,8},{9,1... | collective-permute-start | bytes 12582920 | tf_op jit(solution)/shard_map/ppermute | solution.py:81
  9.5 130.1 %collective-permute-start = (bf16[2,128,4096]{2,1,0:T(8,128)(2,1)}, bf16[2,128,4096]{2,1,0:T(8,128)(2,1)}, u32[]{:S(2)}, u32[]{:S(2)}) collective-permute-start(bf16[2,128,4096]{2,1,0:T(8,128)(2,1)} %get-tuple-element.260), channel_id=1, source_target_pairs={{0,2},{2,0},{1,3},{3,1},{4,6},{6,4},{5,7},{7,5},{8,10},{10,8},{9,1... | collective-permute-start | bytes 6291464 | tf_op jit(solution)/shard_map/ppermute | solution.py:81
  15.7 250.4 %collective-permute-start.10 = (bf16[512,2048]{1,0:T(8,128)(2,1)}, bf16[512,2048]{1,0:T(8,128)(2,1)}, u32[]{:S(2)}, u32[]{:S(2)}) collective-permute-start(bf16[512,2048]{1,0:T(8,128)(2,1)} %convolution_convert_fusion.3), channel_id=1, source_target_pairs={{0,1},{1,0},{2,3},{3,2},{4,5},{5,4},{6,7},{7,6},{8,9},{9,8},{10,11... | collective-permute-start | bytes 6291464 | tf_op jit(solution)/shard_map/ppermute | solution.py:81
  30.9 207.0 %collective-permute-start.4 = (bf16[512,2048]{1,0:T(8,128)(2,1)}, bf16[512,2048]{1,0:T(8,128)(2,1)}, u32[]{:S(2)}, u32[]{:S(2)}) collective-permute-start(bf16[512,2048]{1,0:T(8,128)(2,1)} %fusion.4), channel_id=1, source_target_pairs={{0,1},{1,0},{2,3},{3,2},{4,5},{5,4},{6,7},{7,6},{8,9},{9,8},{10,11... | collective-permute-start | bytes 6291464 | tf_op jit(solution)/shard_map/ppermute | solution.py:81
  139.5 111.7 %collective-permute-start.9 = (bf16[2,128,4096]{2,1,0:T(8,128)(2,1)}, bf16[2,128,4096]{2,1,0:T(8,128)(2,1)}, u32[]{:S(2)}, u32[]{:S(2)}) collective-permute-start(bf16[2,128,4096]{2,1,0:T(8,128)(2,1)} %get-tuple-element.145), channel_id=1, source_target_pairs={{0,2},{2,0},{1,3},{3,1},{4,6},{6,4},{5,7},{7,5},{8,10},{10,8},{9,1... | collective-permute-start | bytes 6291464 | tf_op jit(solution)/shard_map/ppermute | solution.py:81
  166.4 65.1 %collective-permute-start.5 = (bf16[2,128,4096]{2,1,0:T(8,128)(2,1)}, bf16[2,128,4096]{2,1,0:T(8,128)(2,1)S(1)}, u32[]{:S(2)}, u32[]{:S(2)}) collective-permute-start(bf16[2,128,4096]{2,1,0:T(8,128)(2,1)} %get-tuple-element.136), channel_id=1, source_target_pairs={{0,2},{2,0},{1,3},{3,1},{4,6},{6,4},{5,7},{7,5},{8,10},{10,8},{9,1... | collective-permute-start | bytes 6291464 | tf_op jit(solution)/shard_map/ppermute | solution.py:81
  187.9 79.7 %collective-permute-start.11 = (bf16[512,2048]{1,0:T(8,128)(2,1)}, bf16[512,2048]{1,0:T(8,128)(2,1)}, u32[]{:S(2)}, u32[]{:S(2)}) collective-permute-start(bf16[512,2048]{1,0:T(8,128)(2,1)} %convolution_convert_fusion.1), channel_id=1, source_target_pairs={{0,1},{1,0},{2,3},{3,2},{4,5},{5,4},{6,7},{7,6},{8,9},{9,8},{10,11... | collective-permute-start | bytes 6291464 | tf_op jit(solution)/shard_map/ppermute | solution.py:81
  251.2 132.1 %collective-permute-start.21 = (bf16[2,64,4096]{2,1,0:T(8,128)(2,1)}, bf16[2,64,4096]{2,1,0:T(8,128)(2,1)}, u32[]{:S(2)}, u32[]{:S(2)}) collective-permute-start(bf16[2,64,4096]{2,1,0:T(8,128)(2,1)} %get-tuple-element.187), channel_id=1, source_target_pairs={{0,2},{2,0},{1,3},{3,1},{4,6},{6,4},{5,7},{7,5},{8,10},{10,8},{9,1... | collective-permute-start | bytes 3145736 | tf_op jit(solution)/shard_map/ppermute | solution.py:81
  252.3 93.8 %collective-permute-start.16 = (bf16[2,64,4096]{2,1,0:T(8,128)(2,1)}, bf16[2,64,4096]{2,1,0:T(8,128)(2,1)}, u32[]{:S(2)}, u32[]{:S(2)}) collective-permute-start(bf16[2,64,4096]{2,1,0:T(8,128)(2,1)} %get-tuple-element.166), channel_id=1, source_target_pairs={{0,2},{2,0},{1,3},{3,1},{4,6},{6,4},{5,7},{7,5},{8,10},{10,8},{9,1... | collective-permute-start | bytes 3145736 | tf_op jit(solution)/shard_map/ppermute | solution.py:81
  264.3 46.5 %collective-permute-start.8 = (bf16[128,2048]{1,0:T(8,128)(2,1)S(1)}, bf16[128,2048]{1,0:T(8,128)(2,1)S(1)}, u32[]{:S(2)}, u32[]{:S(2)}) collective-permute-start(bf16[128,2048]{1,0:T(8,128)(2,1)S(1)} %add_convert_fusion.6), channel_id=1, source_target_pairs={{0,2},{2,0},{1,3},{3,1},{4,6},{6,4},{5,7},{7,5},{8,10},{10,8},{9,1... | collective-permute-start | bytes 1572872 | tf_op jit(solution)/shard_map/ppermute | solution.py:81
  266.1 51.8 %collective-permute-start.14 = (bf16[128,4096]{1,0:T(8,128)(2,1)S(1)}, bf16[128,4096]{1,0:T(8,128)(2,1)S(1)}, u32[]{:S(2)}, u32[]{:S(2)}) collective-permute-start(bf16[128,4096]{1,0:T(8,128)(2,1)S(1)} %fusion.12), channel_id=1, source_target_pairs={{0,1},{1,0},{2,3},{3,2},{4,5},{5,4},{6,7},{7,6},{8,9},{9,8},{10,11... | collective-permute-start | bytes 3145736 | tf_op jit(solution)/shard_map/ppermute | solution.py:81
  282.9 37.3 %collective-permute-start.13 = (bf16[128,2048]{1,0:T(8,128)(2,1)}, bf16[128,2048]{1,0:T(8,128)(2,1)}, u32[]{:S(2)}, u32[]{:S(2)}) collective-permute-start(bf16[128,2048]{1,0:T(8,128)(2,1)} %convolution_convert_fusion.5), channel_id=1, source_target_pairs={{0,1},{1,0},{2,3},{3,2},{4,5},{5,4},{6,7},{7,6},{8,9},{9,8},{10,11... | collective-permute-start | bytes 1572872 | tf_op jit(solution)/shard_map/ppermute | solution.py:81
  310.9 23.7 %collective-permute-start.29 = (bf16[128,4096]{1,0:T(8,128)(2,1)}, bf16[128,4096]{1,0:T(8,128)(2,1)S(1)}, u32[]{:S(2)}, u32[]{:S(2)}) collective-permute-start(bf16[128,4096]{1,0:T(8,128)(2,1)} %add_convert_fusion.2), channel_id=1, source_target_pairs={{4,0},{8,4},{12,8},{16,12},{20,16},{24,20},{28,24},{0,28},{5,1},{9... | collective-permute-start | bytes 3145736 | tf_op jit(solution)/shard_map/ppermute | solution.py:16
  317.9 20.5 %collective-permute-start.12 = (bf16[128,4096]{1,0:T(8,128)(2,1)S(1)}, bf16[128,4096]{1,0:T(8,128)(2,1)S(1)}, u32[]{:S(2)}, u32[]{:S(2)}) collective-permute-start(bf16[128,4096]{1,0:T(8,128)(2,1)S(1)} %fusion.22), channel_id=1, source_target_pairs={{28,0},{0,4},{4,8},{8,12},{12,16},{16,20},{20,24},{24,28},{29,1},{... | collective-permute-start | bytes 3145736 | tf_op jit(solution)/shard_map/ppermute | solution.py:16
  322.1 34.4 %collective-permute-start.15 = (bf16[128,2048]{1,0:T(8,128)(2,1)}, bf16[128,2048]{1,0:T(8,128)(2,1)}, u32[]{:S(2)}, u32[]{:S(2)}) collective-permute-start(bf16[128,2048]{1,0:T(8,128)(2,1)} %add_convert_fusion.5), channel_id=1, source_target_pairs={{0,2},{2,0},{1,3},{3,1},{4,6},{6,4},{5,7},{7,5},{8,10},{10,8},{9,1... | collective-permute-start | bytes 1572872 | tf_op jit(solution)/shard_map/ppermute | solution.py:81
  339.1 26.2 %collective-permute-start.19 = (bf16[128,4096]{1,0:T(8,128)(2,1)S(1)}, bf16[128,4096]{1,0:T(8,128)(2,1)S(1)}, u32[]{:S(2)}, u32[]{:S(2)}) collective-permute-start(bf16[128,4096]{1,0:T(8,128)(2,1)S(1)} %fusion.15), channel_id=1, source_target_pairs={{0,1},{1,0},{2,3},{3,2},{4,5},{5,4},{6,7},{7,6},{8,9},{9,8},{10,11... | collective-permute-start | bytes 3145736 | tf_op jit(solution)/shard_map/ppermute | solution.py:81
  346.1 24.6 %collective-permute-start.30 = (bf16[128,4096]{1,0:T(8,128)(2,1)}, bf16[128,4096]{1,0:T(8,128)(2,1)S(1)}, u32[]{:S(2)}, u32[]{:S(2)}) collective-permute-start(bf16[128,4096]{1,0:T(8,128)(2,1)} %add_convert_fusion.1), channel_id=1, source_target_pairs={{4,0},{8,4},{12,8},{16,12},{20,16},{24,20},{28,24},{0,28},{5,1},{9... | collective-permute-start | bytes 3145736 | tf_op jit(solution)/shard_map/ppermute | solution.py:16
  350.3 18.7 %collective-permute-start.18 = (bf16[64,2048]{1,0:T(8,128)(2,1)S(1)}, bf16[64,2048]{1,0:T(8,128)(2,1)}, u32[]{:S(2)}, u32[]{:S(2)}) collective-permute-start(bf16[64,2048]{1,0:T(8,128)(2,1)S(1)} %convolution_convert_fusion.13), channel_id=1, source_target_pairs={{0,1},{1,0},{2,3},{3,2},{4,5},{5,4},{6,7},{7,6},{8,9},{9,8},{10,11... | collective-permute-start | bytes 786440 | tf_op jit(solution)/shard_map/ppermute | solution.py:81
  370.0 22.7 %collective-permute-start.20 = (bf16[64,2048]{1,0:T(8,128)(2,1)S(1)}, bf16[64,2048]{1,0:T(8,128)(2,1)}, u32[]{:S(2)}, u32[]{:S(2)}) collective-permute-start(bf16[64,2048]{1,0:T(8,128)(2,1)S(1)} %add_convert_fusion.9), channel_id=1, source_target_pairs={{0,2},{2,0},{1,3},{3,1},{4,6},{6,4},{5,7},{7,5},{8,10},{10,8},{9,1... | collective-permute-start | bytes 786440 | tf_op jit(solution)/shard_map/ppermute | solution.py:81
  376.6 35.3 %collective-permute-start.24 = (bf16[128,4096]{1,0:T(8,128)(2,1)S(1)}, bf16[128,4096]{1,0:T(8,128)(2,1)S(1)}, u32[]{:S(2)}, u32[]{:S(2)}) collective-permute-start(bf16[128,4096]{1,0:T(8,128)(2,1)S(1)} %fusion.18), channel_id=1, source_target_pairs={{0,1},{1,0},{2,3},{3,2},{4,5},{5,4},{6,7},{7,6},{8,9},{9,8},{10,11... | collective-permute-start | bytes 3145736 | tf_op jit(solution)/shard_map/ppermute | solution.py:81
  387.4 25.9 %collective-permute-start.23 = (bf16[64,2048]{1,0:T(8,128)(2,1)S(1)}, bf16[64,2048]{1,0:T(8,128)(2,1)S(1)}, u32[]{:S(2)}, u32[]{:S(2)}) collective-permute-start(bf16[64,2048]{1,0:T(8,128)(2,1)S(1)} %convolution_convert_fusion.11), channel_id=1, source_target_pairs={{0,1},{1,0},{2,3},{3,2},{4,5},{5,4},{6,7},{7,6},{8,9},{9,8},{10,11... | collective-permute-start | bytes 786440 | tf_op jit(solution)/shard_map/ppermute | solution.py:81
  395.2 24.4 %collective-permute-start.31 = (bf16[128,4096]{1,0:T(8,128)(2,1)S(1)}, bf16[128,4096]{1,0:T(8,128)(2,1)S(1)}, u32[]{:S(2)}, u32[]{:S(2)}) collective-permute-start(bf16[128,4096]{1,0:T(8,128)(2,1)S(1)} %copy-done.6), channel_id=1, source_target_pairs={{4,0},{8,4},{12,8},{16,12},{20,16},{24,20},{28,24},{0,28},{5,1},{9... | collective-permute-start | bytes 3145736 | tf_op jit(solution)/shard_map/ppermute | solution.py:16
  437.1 22.4 %collective-permute-start.33 = (bf16[64,4096]{1,0:T(8,128)(2,1)S(1)}, bf16[64,4096]{1,0:T(8,128)(2,1)S(1)}, u32[]{:S(2)}, u32[]{:S(2)}) collective-permute-start(bf16[64,4096]{1,0:T(8,128)(2,1)S(1)} %add_convert_fusion.3), channel_id=1, source_target_pairs={{4,0},{8,4},{12,8},{16,12},{20,16},{24,20},{28,24},{0,28},{5,1},{9... | collective-permute-start | bytes 1572872 | tf_op jit(solution)/shard_map/ppermute | solution.py:16
  438.5 17.7 %collective-permute-start.28 = (bf16[64,4096]{1,0:T(8,128)(2,1)S(1)}, bf16[64,4096]{1,0:T(8,128)(2,1)S(1)}, u32[]{:S(2)}, u32[]{:S(2)}) collective-permute-start(bf16[64,4096]{1,0:T(8,128)(2,1)S(1)} %fusion.31), channel_id=1, source_target_pairs={{0,1},{1,0},{2,3},{3,2},{4,5},{5,4},{6,7},{7,6},{8,9},{9,8},{10,11... | collective-permute-start | bytes 1572872 | tf_op jit(solution)/shard_map/ppermute | solution.py:81
  (29 other events, 569.1 us)

commit v3 on v2

--- a/solution.py
+++ b/solution.py
@@ -132,9 +132,8 @@
 
     def send(c):
         block = paired[:, takes[c]]
-        gate = None if c == 0 else v_far if c == 1 else arrived[c - 2]
-        if gate is not None:
-            block = lax.optimization_barrier((block, gate))[0]
+        if c > 0:
+            block = lax.optimization_barrier((block, gates[c - 1]))[0]
         arrived.append(swapped(block, "dp"))
 
     send(0)
@@ -143,7 +142,9 @@
     mixed_own = order.step(lambda a, b: dot(mine(a), b), rows, w)
     back_own = order.step(lambda a, b: back(mine(a), b), cot, v)
     back_away = swapped(order.step(lambda a, b: back(others(a), b), cot, v_far), "tensor")
+    gates = [v_far, arrived[0], arrived[0]]
     send(1)
+    send(2)
     back_far = order.step(lambda a, b: back(mine(a), b), cot, v_far)
     v_all = order.step(
         lambda a, b: jnp.concatenate([jnp.where(j == 0, a, b), jnp.where(j == 0, b, a)], axis=0), v, v_far
@@ -154,8 +155,9 @@
     def multiply(c):
         half_of = lambda x, i: lax.dynamic_index_in_dim(x, i, 0, keepdims=False)
         summed[c] = swapped(order.step(lambda x: dot(half_of(x, 1 - k), w), arrived[c]), "tensor")
-        if c + 2 < count:
-            send(c + 2)
+        gates.append(arrived[c])
+        if c + 3 < count:
+            send(c + 3)
         kept[c] = order.step(lambda x: dot(half_of(x, k), w), arrived[c])
 
     def give_back(c):
@@ -182,17 +184,15 @@
         normed[c], inv = order.step(norm, stream[c])
         got[c] = swapped(normed[c], "tensor")
 
-        def finish(s, inv, own, own_in, far, far_in, cots):
+        def finish(s, inv, own, own_in, far, cots):
             unit = s.astype(f32) * inv
-            grad = halves(add(own[t], own_in[t]), add(far[t], far_in[t]))
+            grad = halves(add(own[t], own_in[t]), far[t])
             gains = jnp.sum(grad * unit, axis=0)
             weighted = gain_row * grad
             centre = jnp.mean(weighted * unit, axis=-1, keepdims=True)
             return (cots[t].astype(f32) + inv * (weighted - unit * centre)).astype(bf16), gains
 
-        out, gains = order.step(
-            finish, stream[c], inv, back_own, back_near, back_far, back_away, cot_stream
-        )
+        out, gains = order.step(finish, stream[c], inv, back_own, back_near, grad_far, cot_stream)
         gain_part = gains if gain_part is None else gain_part + gains
         grads[c] = shifted(out, "pipe", -1)
 
@@ -200,20 +200,23 @@
         near[c] = order.step(dot, normed[c], v_all)
         across[c] = order.step(dot, got[c], v_all)
 
-    for i in range(count + 2):
+    for i in range(count + 3):
         if i < count:
             multiply(i)
-        if 1 <= i <= count:
-            finish_stream(i - 1)
-        if 2 <= i:
-            project(i - 2)
+        if i == 1:
+            grad_far = order.step(add, back_far, back_away)
+        if 3 <= i:
+            project(i - 3)
+        if 2 <= i <= count + 1:
+            normalise(i - 2)
         if i < count:
             give_back(i)
         if 1 <= i <= count:
-            normalise(i - 1)
-            if i == count:
-                gain_part = gain_part + swapped(gain_part, "tensor")
-                gain_part = gain_part + swapped(gain_part, "dp")
+            finish_stream(i - 1)
+    beside = swapped(gain_part, "tensor")
+    across_y = swapped(gain_part, "dp")
+    opposite = lax.ppermute(gain_part, ("dp", "tensor"), [(i, 3 - i) for i in range(4)])
+    gain_part = (gain_part + beside) + (across_y + opposite)
 
     def joined(parts):
         return jnp.concatenate([parts[c] for c in range(count)], 0)

time: 468 us -> 453 us (0.968)
  waiting for transfers between devices: 220 us -> 202 us
  starting transfers between devices: 39.6 us -> 47.7 us
  other arithmetic: 60.4 us -> 55.1 us
    ppermute x10, waiting for transfers between devices: 44.3 us -> 24.2 us  [shifted(): return lax.ppermute(block, axis, route)]
  transfers between devices with their start and end apart: 36 -> 37, of which waited for: 16 -> 9; matrix products, arithmetic and copies ran while one was open for 42% -> 43% of each run, Pallas kernels for 0% -> 0%
where the time goes in v3:
time: 453 us; the launch traced here: 445 us
  waiting for transfers between devices  202 us (45%)
  matrix products  120 us (26%)
  other arithmetic  55.1 us (12%)
  starting transfers between devices  47.7 us (11%)
  local copies, waits for them, and re-layouts  18.1 us (4%)
    ppermute x26, waiting for transfers between devices, swapped(): return lax.ppermute(block, axis, [(0, 1), (1, 0)])  178 us
    dot_general x22, matrix products, dot(): return jnp.dot(a, b, preferred_element_type=f32).astype(bf16)  95.8 us
    ppermute x26, starting transfers between devices, swapped(): return lax.ppermute(block, axis, [(0, 1), (1, 0)])  32.9 us
    ppermute x10, waiting for transfers between devices, shifted(): return lax.ppermute(block, axis, route)  24.2 us
    dot_general x4, matrix products, back(): lax.dot_general(a, b, (((1,), (1,)), ((), ())), preferred_element_type=f32)  23.9 us
    ppermute x10, starting transfers between devices, shifted(): return lax.ppermute(block, axis, route)  14.1 us
    select_n x10, other arithmetic, halves(): jnp.where(j == 0, own, far)  13.4 us
  transfers between devices with their start and end apart: 37, of which 9 were waited for; matrix products, arithmetic and copies ran while one was open for 43% of the time, Pallas kernels for 0%

profile of v3, /device:TPU:0, one launch (start us, length us, event | category | flops | bytes accessed | tf_op | source)
XLA Modules:
  0.0 444.6 jit_solution(4113077174736218698)
XLA Ops:
  3.7 5.8 %fusion.104 = (bf16[2,128,4096]{2,1,0:T(8,128)(2,1)}, bf16[2,128,4096]{2,1,0:T(8,128)(2,1)}, bf16[2,128,4096]{2,1,0:T(8,128)(2,1)}) fusion(bf16[2,512,4096]{2,1,0:T(8,128)(2,1)} %bitcast.117), kind=kLoop, calls=%fused_computation.227 | loop fusion | bytes 12582912 | tf_op jit(solution)/shard_map/slice | solution.py:134
  9.6 6.1 %convolution_convert_fusion.3 = bf16[512,2048]{1,0:T(8,128)(2,1)} fusion(bf16[1,1,1024,1024]{3,2,1,0:T(8,128)(2,1)S(1)} %copy-done, s32[]{:T(128)S(6)} %select_n.139, bf16[1,2048,1024]{2,1,0:T(8,128)(2,1)} %param.9), kind=kOutput, calls=%fused_computation.13 | convolution fusion | flops 2148532224 | bytes 7340036 | tf_op jit(solution)/shard_map/dot_general | solution.py:119
  17.6 13.4 %fusion.4 = bf16[512,2048]{1,0:T(8,128)(2,1)} fusion(bf16[4096,2048]{1,0:T(8,128)(2,1)} %bitcast.111, bf16[1024,4096]{1,0:T(8,128)(2,1)S(1)} %bitcast.120, s32[]{:T(128)S(6)} %select_n.139), kind=kOutput, calls=%fused_computation.8 | convolution fusion | flops 8590983168 | bytes 23068676 | tf_op jit(solution)/shard_map/dot_general | solution.py:116
  31.1 14.7 %fusion.7 = bf16[512,2048]{1,0:T(8,128)(2,1)} fusion(bf16[4096,2048]{1,0:T(8,128)(2,1)} %bitcast.112, bf16[1024,4096]{1,0:T(8,128)(2,1)} %bitcast.118, s32[]{:T(128)S(6)} %select_n.140), kind=kOutput, calls=%fused_computation.9 | convolution fusion | flops 8590983168 | bytes 23068676 | tf_op jit(solution)/shard_map/dot_general | solution.py:116
  45.8 5.9 %convolution_convert_fusion.2 = bf16[512,2048]{1,0:T(8,128)(2,1)} fusion(bf16[2048,1024]{1,0:T(8,128)(2,1)} %bitcast.122, bf16[1024,1024]{1,0:T(8,128)(2,1)S(1)} %bitcast.108, s32[]{:T(128)S(6)} %select_n.140), kind=kOutput, calls=%fused_computation.12 | convolution fusion | flops 2148532224 | bytes 7340036 | tf_op jit(solution)/shard_map/dot_general | solution.py:119
  54.8 84.7 %collective-permute-done = bf16[2,128,4096]{2,1,0:T(8,128)(2,1)} collective-permute-done((bf16[2,128,4096]{2,1,0:T(8,128)(2,1)}, bf16[2,128,4096]{2,1,0:T(8,128)(2,1)}, u32[]{:S(2)}, u32[]{:S(2)}) %collective-permute-start) | collective-permute-done | bytes 2097184 | tf_op jit(solution)/shard_map/ppermute | solution.py:81
  141.3 5.9 %convolution_convert_fusion.1 = bf16[512,2048]{1,0:T(8,128)(2,1)} fusion(bf16[2048,1024]{1,0:T(8,128)(2,1)} %collective-permute-done.1, bf16[1024,1024]{1,0:T(8,128)(2,1)S(1)} %bitcast.109, s32[]{:T(128)S(6)} %select_n.139), kind=kOutput, calls=%fused_computation.11 | convolution fusion | flops 2148532224 | bytes 7340036 | tf_op jit(solution)/shard_map/dot_general | solution.py:119
  147.1 6.1 %convolution_convert_fusion = bf16[512,2048]{1,0:T(8,128)(2,1)} fusion(bf16[2048,1024]{1,0:T(8,128)(2,1)} %collective-permute-done.1, bf16[1024,1024]{1,0:T(8,128)(2,1)S(1)} %bitcast.110, s32[]{:T(128)S(6)} %select_n.140), kind=kOutput, calls=%fused_computation.10 | convolution fusion | flops 2148532224 | bytes 7340036 | tf_op jit(solution)/shard_map/dot_general | solution.py:119
  153.2 5.4 %broadcast_select_fusion.1 = (bf16[2048,1024]{1,0:T(8,128)(2,1)}, bf16[2048,1024]{1,0:T(8,128)(2,1)}) fusion(bf16[2048,1024]{1,0:T(8,128)(2,1)S(1)} %bitcast.123, bf16[2048,1024]{1,0:T(8,128)(2,1)} %collective-permute-done.1, pred[]{:T(512)S(6)} %eq.4), kind=kLoop, calls=%fused_computation.7 | loop fusion | flops 4194304 | bytes 16777216 | tf_op jit(solution)/shard_map/jit(_where)/select_n | solution.py:150
  158.6 7.7 %pad_maximum_fusion = bf16[4096,1024]{1,0:T(8,128)(2,1)} fusion(bf16[2048,1024]{1,0:T(8,128)(2,1)} %get-tuple-element.256, bf16[2048,1024]{1,0:T(8,128)(2,1)} %get-tuple-element.255), kind=kLoop, calls=%fused_computation | loop fusion | flops 16777216 | bytes 16777216 | tf_op jit(solution)/shard_map/concatenate | solution.py:150
  166.6 8.6 %convolution_convert_fusion.9 = bf16[128,2048]{1,0:T(8,128)(2,1)S(1)} fusion(bf16[2,128,4096]{2,1,0:T(8,128)(2,1)} %collective-permute-done, s32[]{:T(128)S(6)} %select_n.143, bf16[1,4096,2048]{2,1,0:T(8,128)(2,1)} %param.8), kind=kOutput, calls=%fused_computation.25 | convolution fusion | flops 2147745792 | bytes 18350084 | tf_op jit(solution)/shard_map/dot_general | solution.py:116
  177.0 9.2 %convolution_convert_fusion.8 = bf16[128,2048]{1,0:T(8,128)(2,1)S(1)} fusion(bf16[2,128,4096]{2,1,0:T(8,128)(2,1)} %collective-permute-done, s32[]{:T(128)S(6)} %select_n.144, bf16[1,4096,2048]{2,1,0:T(8,128)(2,1)} %param.8), kind=kOutput, calls=%fused_computation.24 | convolution fusion | flops 2147745792 | bytes 18350084 | tf_op jit(solution)/shard_map/dot_general | solution.py:116
  189.4 42.1 %collective-permute-done.5 = bf16[2,128,4096]{2,1,0:T(8,128)(2,1)S(1)} collective-permute-done((bf16[2,128,4096]{2,1,0:T(8,128)(2,1)}, bf16[2,128,4096]{2,1,0:T(8,128)(2,1)S(1)}, u32[]{:S(2)}, u32[]{:S(2)}) %collective-permute-start.5) | collective-permute-done | bytes 2097184 | tf_op jit(solution)/shard_map/ppermute | solution.py:81
  240.3 9.3 %collective-permute-done.6 = bf16[128,2048]{1,0:T(8,128)(2,1)S(1)} collective-permute-done((bf16[128,2048]{1,0:T(8,128)(2,1)S(1)}, bf16[128,2048]{1,0:T(8,128)(2,1)S(1)}, u32[]{:S(2)}, u32[]{:S(2)}) %collective-permute-start.6) | collective-permute-done | bytes 524320 | tf_op jit(solution)/shard_map/ppermute | solution.py:81
  253.9 3.8 convolution_convert_fusion.5
  263.0 6.9 %collective-permute-done.8 = bf16[128,4096]{1,0:T(8,128)(2,1)S(1)} collective-permute-done((bf16[128,4096]{1,0:T(8,128)(2,1)S(1)}, bf16[128,4096]{1,0:T(8,128)(2,1)S(1)}, u32[]{:S(2)}, u32[]{:S(2)}) %collective-permute-start.8) | collective-permute-done | bytes 1048608 | tf_op jit(solution)/shard_map/ppermute | solution.py:16
  281.4 28.2 %collective-permute-done.9 = bf16[128,2048]{1,0:T(8,128)(2,1)S(1)} collective-permute-done((bf16[128,2048]{1,0:T(8,128)(2,1)S(1)}, bf16[128,2048]{1,0:T(8,128)(2,1)S(1)}, u32[]{:S(2)}, u32[]{:S(2)}) %collective-permute-start.9) | collective-permute-done | bytes 524320 | tf_op jit(solution)/shard_map/ppermute | solution.py:81
  312.3 4.3 convolution_convert_fusion.13
  318.2 4.1 convolution_convert_fusion.12
  347.8 4.1 convolution_convert_fusion.11
  353.1 4.1 convolution_convert_fusion.10
  383.9 8.9 %collective-permute-done.23 = bf16[64,4096]{1,0:T(8,128)(2,1)S(1)} collective-permute-done((bf16[64,4096]{1,0:T(8,128)(2,1)S(1)}, bf16[64,4096]{1,0:T(8,128)(2,1)S(1)}, u32[]{:S(2)}, u32[]{:S(2)}) %collective-permute-start.23) | collective-permute-done | bytes 524320 | tf_op jit(solution)/shard_map/ppermute | solution.py:16
  407.7 8.4 %collective-permute-done.26 = bf16[64,4096]{1,0:T(8,128)(2,1)S(1)} collective-permute-done((bf16[64,4096]{1,0:T(8,128)(2,1)S(1)}, bf16[64,4096]{1,0:T(8,128)(2,1)S(1)}, u32[]{:S(2)}, u32[]{:S(2)}) %collective-permute-start.26) | collective-permute-done | bytes 524320 | tf_op jit(solution)/shard_map/ppermute | solution.py:16
  426.9 12.0 %collective-permute-done.28 = bf16[64,4096]{1,0:T(8,128)(2,1)S(1)} collective-permute-done((bf16[64,4096]{1,0:T(8,128)(2,1)S(1)}, bf16[64,4096]{1,0:T(8,128)(2,1)S(1)}, u32[]{:S(2)}, u32[]{:S(2)}) %collective-permute-start.28) | collective-permute-done | bytes 524320 | tf_op jit(solution)/shard_map/ppermute | solution.py:81
  (187 shorter events, 133.2 us)
Async XLA Ops:
  0.6 140.6 %collective-permute-start.1 = (bf16[2048,1024]{1,0:T(8,128)(2,1)}, bf16[2048,1024]{1,0:T(8,128)(2,1)}, u32[]{:S(2)}, u32[]{:S(2)}) collective-permute-start(bf16[2048,1024]{1,0:T(8,128)(2,1)} %bitcast.121), channel_id=1, source_target_pairs={{0,2},{2,0},{1,3},{3,1},{4,6},{6,4},{5,7},{7,5},{8,10},{10,8},{9,1... | collective-permute-start | bytes 12582920 | tf_op jit(solution)/shard_map/ppermute | solution.py:81
  9.5 130.1 %collective-permute-start = (bf16[2,128,4096]{2,1,0:T(8,128)(2,1)}, bf16[2,128,4096]{2,1,0:T(8,128)(2,1)}, u32[]{:S(2)}, u32[]{:S(2)}) collective-permute-start(bf16[2,128,4096]{2,1,0:T(8,128)(2,1)} %get-tuple-element.254), channel_id=1, source_target_pairs={{0,2},{2,0},{1,3},{3,1},{4,6},{6,4},{5,7},{7,5},{8,10},{10,8},{9,1... | collective-permute-start | bytes 6291464 | tf_op jit(solution)/shard_map/ppermute | solution.py:81
  15.7 256.9 %collective-permute-start.12 = (bf16[512,2048]{1,0:T(8,128)(2,1)}, bf16[512,2048]{1,0:T(8,128)(2,1)}, u32[]{:S(2)}, u32[]{:S(2)}) collective-permute-start(bf16[512,2048]{1,0:T(8,128)(2,1)} %convolution_convert_fusion.3), channel_id=1, source_target_pairs={{0,1},{1,0},{2,3},{3,2},{4,5},{5,4},{6,7},{7,6},{8,9},{9,8},{10,11... | collective-permute-start | bytes 6291464 | tf_op jit(solution)/shard_map/ppermute | solution.py:81
  31.0 219.7 %collective-permute-start.4 = (bf16[512,2048]{1,0:T(8,128)(2,1)}, bf16[512,2048]{1,0:T(8,128)(2,1)}, u32[]{:S(2)}, u32[]{:S(2)}) collective-permute-start(bf16[512,2048]{1,0:T(8,128)(2,1)} %fusion.4), channel_id=1, source_target_pairs={{0,1},{1,0},{2,3},{3,2},{4,5},{5,4},{6,7},{7,6},{8,9},{9,8},{10,11... | collective-permute-start | bytes 6291464 | tf_op jit(solution)/shard_map/ppermute | solution.py:81
  139.5 114.4 %collective-permute-start.10 = (bf16[2,128,4096]{2,1,0:T(8,128)(2,1)}, bf16[2,128,4096]{2,1,0:T(8,128)(2,1)}, u32[]{:S(2)}, u32[]{:S(2)}) collective-permute-start(bf16[2,128,4096]{2,1,0:T(8,128)(2,1)} %get-tuple-element.144), channel_id=1, source_target_pairs={{0,2},{2,0},{1,3},{3,1},{4,6},{6,4},{5,7},{7,5},{8,10},{10,8},{9,1... | collective-permute-start | bytes 6291464 | tf_op jit(solution)/shard_map/ppermute | solution.py:81
  166.3 65.1 %collective-permute-start.5 = (bf16[2,128,4096]{2,1,0:T(8,128)(2,1)}, bf16[2,128,4096]{2,1,0:T(8,128)(2,1)S(1)}, u32[]{:S(2)}, u32[]{:S(2)}) collective-permute-start(bf16[2,128,4096]{2,1,0:T(8,128)(2,1)} %get-tuple-element.133), channel_id=1, source_target_pairs={{0,2},{2,0},{1,3},{3,1},{4,6},{6,4},{5,7},{7,5},{8,10},{10,8},{9,1... | collective-permute-start | bytes 6291464 | tf_op jit(solution)/shard_map/ppermute | solution.py:81
  187.9 50.1 %collective-permute-start.7 = (bf16[512,2048]{1,0:T(8,128)(2,1)S(1)}, bf16[512,2048]{1,0:T(8,128)(2,1)S(1)}, u32[]{:S(2)}, u32[]{:S(2)}) collective-permute-start(bf16[512,2048]{1,0:T(8,128)(2,1)S(1)} %copy-done.13), channel_id=1, source_target_pairs={{0,1},{1,0},{2,3},{3,2},{4,5},{5,4},{6,7},{7,6},{8,9},{9,8},{10,11... | collective-permute-start | bytes 6291464 | tf_op jit(solution)/shard_map/ppermute | solution.py:81
  249.6 62.7 %collective-permute-start.15 = (bf16[2,64,4096]{2,1,0:T(8,128)(2,1)}, bf16[2,64,4096]{2,1,0:T(8,128)(2,1)}, u32[]{:S(2)}, u32[]{:S(2)}) collective-permute-start(bf16[2,64,4096]{2,1,0:T(8,128)(2,1)} %get-tuple-element.160), channel_id=1, source_target_pairs={{0,2},{2,0},{1,3},{3,1},{4,6},{6,4},{5,7},{7,5},{8,10},{10,8},{9,1... | collective-permute-start | bytes 3145736 | tf_op jit(solution)/shard_map/ppermute | solution.py:81
  250.7 97.1 %collective-permute-start.20 = (bf16[2,64,4096]{2,1,0:T(8,128)(2,1)}, bf16[2,64,4096]{2,1,0:T(8,128)(2,1)}, u32[]{:S(2)}, u32[]{:S(2)}) collective-permute-start(bf16[2,64,4096]{2,1,0:T(8,128)(2,1)} %get-tuple-element.180), channel_id=1, source_target_pairs={{0,2},{2,0},{1,3},{3,1},{4,6},{6,4},{5,7},{7,5},{8,10},{10,8},{9,1... | collective-permute-start | bytes 3145736 | tf_op jit(solution)/shard_map/ppermute | solution.py:81
  257.7 21.3 %collective-permute-start.11 = (bf16[128,2048]{1,0:T(8,128)(2,1)S(1)}, bf16[128,2048]{1,0:T(8,128)(2,1)}, u32[]{:S(2)}, u32[]{:S(2)}) collective-permute-start(bf16[128,2048]{1,0:T(8,128)(2,1)S(1)} %convolution_convert_fusion.5), channel_id=1, source_target_pairs={{0,1},{1,0},{2,3},{3,2},{4,5},{5,4},{6,7},{7,6},{8,9},{9,8},{10,11... | collective-permute-start | bytes 1572872 | tf_op jit(solution)/shard_map/ppermute | solution.py:81
  269.9 39.7 %collective-permute-start.9 = (bf16[128,2048]{1,0:T(8,128)(2,1)S(1)}, bf16[128,2048]{1,0:T(8,128)(2,1)S(1)}, u32[]{:S(2)}, u32[]{:S(2)}) collective-permute-start(bf16[128,2048]{1,0:T(8,128)(2,1)S(1)} %add_convert_fusion.6), channel_id=1, source_target_pairs={{0,2},{2,0},{1,3},{3,1},{4,6},{6,4},{5,7},{7,5},{8,10},{10,8},{9,1... | collective-permute-start | bytes 1572872 | tf_op jit(solution)/shard_map/ppermute | solution.py:81
  272.6 54.1 %collective-permute-start.17 = (bf16[128,4096]{1,0:T(8,128)(2,1)}, bf16[128,4096]{1,0:T(8,128)(2,1)}, u32[]{:S(2)}, u32[]{:S(2)}) collective-permute-start(bf16[128,4096]{1,0:T(8,128)(2,1)} %fusion.12), channel_id=1, source_target_pairs={{0,1},{1,0},{2,3},{3,2},{4,5},{5,4},{6,7},{7,6},{8,9},{9,8},{10,11... | collective-permute-start | bytes 3145736 | tf_op jit(solution)/shard_map/ppermute | solution.py:81
  280.2 63.3 %collective-permute-start.14 = (bf16[128,2048]{1,0:T(8,128)(2,1)S(1)}, bf16[128,2048]{1,0:T(8,128)(2,1)}, u32[]{:S(2)}, u32[]{:S(2)}) collective-permute-start(bf16[128,2048]{1,0:T(8,128)(2,1)S(1)} %add_convert_fusion.5), channel_id=1, source_target_pairs={{0,2},{2,0},{1,3},{3,1},{4,6},{6,4},{5,7},{7,5},{8,10},{10,8},{9,1... | collective-permute-start | bytes 1572872 | tf_op jit(solution)/shard_map/ppermute | solution.py:81
  312.2 21.1 %collective-permute-start.13 = (bf16[128,4096]{1,0:T(8,128)(2,1)}, bf16[128,4096]{1,0:T(8,128)(2,1)S(1)}, u32[]{:S(2)}, u32[]{:S(2)}) collective-permute-start(bf16[128,4096]{1,0:T(8,128)(2,1)} %fusion.22), channel_id=1, source_target_pairs={{28,0},{0,4},{4,8},{8,12},{12,16},{16,20},{20,24},{24,28},{29,1},{... | collective-permute-start | bytes 3145736 | tf_op jit(solution)/shard_map/ppermute | solution.py:16
  316.6 24.0 %collective-permute-start.16 = (bf16[64,2048]{1,0:T(8,128)(2,1)S(1)}, bf16[64,2048]{1,0:T(8,128)(2,1)}, u32[]{:S(2)}, u32[]{:S(2)}) collective-permute-start(bf16[64,2048]{1,0:T(8,128)(2,1)S(1)} %convolution_convert_fusion.13), channel_id=1, source_target_pairs={{0,1},{1,0},{2,3},{3,2},{4,5},{5,4},{6,7},{7,6},{8,9},{9,8},{10,11... | collective-permute-start | bytes 786440 | tf_op jit(solution)/shard_map/ppermute | solution.py:81
  326.7 30.5 %collective-permute-start.29 = (bf16[128,4096]{1,0:T(8,128)(2,1)}, bf16[128,4096]{1,0:T(8,128)(2,1)}, u32[]{:S(2)}, u32[]{:S(2)}) collective-permute-start(bf16[128,4096]{1,0:T(8,128)(2,1)} %add_convert_fusion.2), channel_id=1, source_target_pairs={{4,0},{8,4},{12,8},{16,12},{20,16},{24,20},{28,24},{0,28},{5,1},{9... | collective-permute-start | bytes 3145736 | tf_op jit(solution)/shard_map/ppermute | solution.py:16
  334.8 30.7 %collective-permute-start.22 = (bf16[128,4096]{1,0:T(8,128)(2,1)}, bf16[128,4096]{1,0:T(8,128)(2,1)}, u32[]{:S(2)}, u32[]{:S(2)}) collective-permute-start(bf16[128,4096]{1,0:T(8,128)(2,1)} %fusion.15), channel_id=1, source_target_pairs={{0,1},{1,0},{2,3},{3,2},{4,5},{5,4},{6,7},{7,6},{8,9},{9,8},{10,11... | collective-permute-start | bytes 3145736 | tf_op jit(solution)/shard_map/ppermute | solution.py:81
  342.4 32.0 %collective-permute-start.19 = (bf16[64,2048]{1,0:T(8,128)(2,1)}, bf16[64,2048]{1,0:T(8,128)(2,1)}, u32[]{:S(2)}, u32[]{:S(2)}) collective-permute-start(bf16[64,2048]{1,0:T(8,128)(2,1)} %add_convert_fusion.9), channel_id=1, source_target_pairs={{0,2},{2,0},{1,3},{3,1},{4,6},{6,4},{5,7},{7,5},{8,10},{10,8},{9,1... | collective-permute-start | bytes 786440 | tf_op jit(solution)/shard_map/ppermute | solution.py:81
  351.9 21.4 %collective-permute-start.21 = (bf16[64,2048]{1,0:T(8,128)(2,1)S(1)}, bf16[64,2048]{1,0:T(8,128)(2,1)}, u32[]{:S(2)}, u32[]{:S(2)}) collective-permute-start(bf16[64,2048]{1,0:T(8,128)(2,1)S(1)} %convolution_convert_fusion.11), channel_id=1, source_target_pairs={{0,1},{1,0},{2,3},{3,2},{4,5},{5,4},{6,7},{7,6},{8,9},{9,8},{10,11... | collective-permute-start | bytes 786440 | tf_op jit(solution)/shard_map/ppermute | solution.py:81
  357.3 26.6 %collective-permute-start.30 = (bf16[128,4096]{1,0:T(8,128)(2,1)}, bf16[128,4096]{1,0:T(8,128)(2,1)S(1)}, u32[]{:S(2)}, u32[]{:S(2)}) collective-permute-start(bf16[128,4096]{1,0:T(8,128)(2,1)} %add_convert_fusion.1), channel_id=1, source_target_pairs={{4,0},{8,4},{12,8},{16,12},{20,16},{24,20},{28,24},{0,28},{5,1},{9... | collective-permute-start | bytes 3145736 | tf_op jit(solution)/shard_map/ppermute | solution.py:16
  369.3 24.3 %collective-permute-start.25 = (bf16[128,4096]{1,0:T(8,128)(2,1)S(1)}, bf16[128,4096]{1,0:T(8,128)(2,1)S(1)}, u32[]{:S(2)}, u32[]{:S(2)}) collective-permute-start(bf16[128,4096]{1,0:T(8,128)(2,1)S(1)} %fusion.18), channel_id=1, source_target_pairs={{0,1},{1,0},{2,3},{3,2},{4,5},{5,4},{6,7},{7,6},{8,9},{9,8},{10,11... | collective-permute-start | bytes 3145736 | tf_op jit(solution)/shard_map/ppermute | solution.py:81
  376.9 21.6 %collective-permute-start.24 = (bf16[64,2048]{1,0:T(8,128)(2,1)S(1)}, bf16[64,2048]{1,0:T(8,128)(2,1)S(1)}, u32[]{:S(2)}, u32[]{:S(2)}) collective-permute-start(bf16[64,2048]{1,0:T(8,128)(2,1)S(1)} %add_convert_fusion.8), channel_id=1, source_target_pairs={{0,2},{2,0},{1,3},{3,1},{4,6},{6,4},{5,7},{7,5},{8,10},{10,8},{9,1... | collective-permute-start | bytes 786440 | tf_op jit(solution)/shard_map/ppermute | solution.py:81
  378.0 26.4 %collective-permute-start.31 = (bf16[128,4096]{1,0:T(8,128)(2,1)S(1)}, bf16[128,4096]{1,0:T(8,128)(2,1)S(1)}, u32[]{:S(2)}, u32[]{:S(2)}) collective-permute-start(bf16[128,4096]{1,0:T(8,128)(2,1)S(1)} %add_convert_fusion), channel_id=1, source_target_pairs={{4,0},{8,4},{12,8},{16,12},{20,16},{24,20},{28,24},{0,28},{5,1},{9... | collective-permute-start | bytes 3145736 | tf_op jit(solution)/shard_map/ppermute | solution.py:16
  400.9 23.6 %collective-permute-start.32 = (bf16[64,4096]{1,0:T(8,128)(2,1)S(1)}, bf16[64,4096]{1,0:T(8,128)(2,1)S(1)}, u32[]{:S(2)}, u32[]{:S(2)}) collective-permute-start(bf16[64,4096]{1,0:T(8,128)(2,1)S(1)} %add_convert_fusion.4), channel_id=1, source_target_pairs={{4,0},{8,4},{12,8},{16,12},{20,16},{24,20},{28,24},{0,28},{5,1},{9... | collective-permute-start | bytes 1572872 | tf_op jit(solution)/shard_map/ppermute | solution.py:16
  (33 other events, 528.0 us)
